TPU v7x, 256 devices: a whole 4x4x8 slice. The times are simulated.
256 devices in a mesh: seq: 32 (over z, y), head: 8 (over x, core).
Axes of the slice: x: 4, y: 4, z: 8, core: 2. Of those that a mesh axis runs over, the one named last changes fastest.
Arguments:
- lengths: int32 [32], replicated, may hold values from 1 to 16384, as said below
- block_table: int32 [32, 256], replicated, may hold values from 0 to 2047, as said below
- slot_request: int32 [32], replicated, may hold values from 0 to 31, each once
- kv_pool: bfloat16 [2048, 64, 8, 256], P('seq', None, 'head'), may hold values from -4 to 4
- new_kv: bfloat16 [3, 32, 8, 256], P(None, 'seq', 'head'), may hold values from -4 to 4
- queries: bfloat16 [2, 32, 8, 1024], P(None, 'seq', 'head'), may hold values from -20 to 20
- residual: bfloat16 [2, 32, 16384], P(None, None, 'seq'), may hold values from -32 to 32
- norm_gain: float32 [16384], P('seq'), may hold values from 0.1 to 1.9
- w_out: bfloat16 [8, 1024, 16384], P('head', None, 'seq'), may hold values from -0.0625 to 0.0625
- w_gate: bfloat16 [26624, 16384], P(('seq', 'head')), may hold values from -0.046875 to 0.046875
- w_up: bfloat16 [26624, 16384], P(('seq', 'head')), may hold values from -0.046875 to 0.046875
- w_down: bfloat16 [26624, 16384], P(('seq', 'head')), may hold values from -0.15625 to 0.15625
Outputs:
- layer_out: bfloat16 [2, 32, 16384], P(None, None, ('seq', 'head'))
Inputs may be any that keep to these rules, and one draw needn't show every extreme that they name: `lengths`: the longest request has exactly 16384 tokens; the pages of all requests together number 2048. `block_table`: for j below request r's page count, entry [r, j] is the pool slot of its page j. Numbering the pages of all requests in order (request r's pages start at O_r, the pages of the requests before r), page O_r + j lies on shard (O_r + j) mod 32, that is in a slot from ((O_r + j) mod 32) * 64 on; every slot holds one page; within a shard the slots are in no order. Entries past the page count are 0.
All inputs are finite; a program needn't handle non-finite values.
Results may differ from a plain program's by a relative error of at most 0.012.
Values may be sent and summed in bfloat16 or wider, within the bound.
A program may use at most 128 MiB of HBM per device.

v0:
```python
import math

import jax
import jax.numpy as jnp
from jax import lax
from jax.sharding import PartitionSpec as P

epsilon = 1e-05


def contract(left_rows, right_rows):
    return lax.dot_general(
        left_rows, right_rows, (((1,), (1,)), ((), ())), preferred_element_type=jnp.float32
    )


def shards(
    lengths,
    block_table,
    slot_request,
    kv_pool,
    new_kv,
    queries,
    residual,
    norm_gain,
    w_out,
    w_gate,
    w_up,
    w_down,
):
    shard_count = lax.axis_size("seq")
    head_count = lax.axis_size("head")
    shard_index = lax.axis_index("seq")
    head_index = lax.axis_index("head")
    slots_here = kv_pool.shape[0]
    page_size = kv_pool.shape[1]
    pair_width = kv_pool.shape[3]
    head_dim = pair_width // 2
    steps_count = queries.shape[0]
    batch_here = queries.shape[1]
    group_width = queries.shape[3]
    group_size = group_width // head_dim
    request_count = lengths.shape[0]
    table_width = block_table.shape[1]
    per_shard = table_width // shard_count
    fresh_count = new_kv.shape[0]
    score_scale = 1.0 / math.sqrt(head_dim)
    page_count = (lengths + page_size - 1) // page_size
    offsets = jnp.cumsum(page_count) - page_count
    fresh_mask = jnp.arange(fresh_count)[None, :] <= jnp.arange(steps_count)[:, None] + 1
    pool_pages = kv_pool.reshape(slots_here, page_size, pair_width)
    w_local = w_out.reshape(group_width, w_out.shape[2])

    def page_numbers(requests, source):
        first_page = (source - offsets[requests]) % shard_count
        return first_page[..., None] + shard_count * jnp.arange(per_shard)

    def weighted(scores, row_peak, values, pattern):
        weights = jnp.exp(scores - row_peak[..., None]).astype(jnp.bfloat16)
        mixed_values = jnp.einsum(pattern, weights, values, preferred_element_type=jnp.float32)
        return (mixed_values, jnp.sum(weights.astype(jnp.float32), -1))

    dest_requests = slot_request.reshape(shard_count, batch_here).T
    capped = jnp.minimum(page_numbers(dest_requests, shard_index), table_width - 1)
    located = block_table[dest_requests[..., None], capped] - shard_index * slots_here
    outgoing = pool_pages[jnp.clip(located, 0, slots_here - 1)]
    arrived = lax.all_to_all(outgoing, "seq", split_axis=1, concat_axis=1, tiled=True)
    my_requests = lax.dynamic_slice_in_dim(slot_request, shard_index * batch_here, batch_here)
    numbers = page_numbers(my_requests[:, None], jnp.arange(shard_count)[None, :])
    positions = numbers[..., None] * page_size + jnp.arange(page_size)
    valid_keys = (positions < lengths[my_requests][:, None, None, None]).reshape(batch_here, -1)
    flat_pages = arrived.reshape(batch_here, -1, pair_width)
    grouped_query = queries.reshape(steps_count, batch_here, group_size, head_dim)
    fresh_rows = new_kv.reshape(fresh_count, batch_here, pair_width)
    raw_scores = (
        jnp.einsum(
            "tbgd,bnd->btgn",
            grouped_query,
            flat_pages[..., :head_dim],
            preferred_element_type=jnp.float32,
        )
        * score_scale
    )
    cached = jnp.where(valid_keys[:, None, None, :], raw_scores, -jnp.inf)
    raw_scores = (
        jnp.einsum(
            "tbgd,ebd->btge",
            grouped_query,
            fresh_rows[..., :head_dim],
            preferred_element_type=jnp.float32,
        )
        * score_scale
    )
    recent = jnp.where(fresh_mask[None, :, None, :], raw_scores, -jnp.inf)
    row_peak = jnp.maximum(jnp.max(cached, -1), jnp.max(recent, -1))
    cached_mix, cached_weight = weighted(
        cached, row_peak, flat_pages[..., head_dim:], "btgn,bnd->btgd"
    )
    recent_mix, recent_weight = weighted(
        recent, row_peak, fresh_rows[..., head_dim:], "btge,ebd->btgd"
    )
    attended = ((cached_mix + recent_mix) / (cached_weight + recent_weight)[..., None]).astype(
        jnp.bfloat16
    )
    attended = attended.transpose(1, 0, 2, 3).reshape(steps_count, batch_here, group_width)
    head_part = jnp.einsum(
        "tbf,fd->tbd",
        lax.all_gather(attended, "seq", axis=1, tiled=True),
        w_local,
        preferred_element_type=jnp.float32,
    )
    attended_sum = lax.psum(head_part, "head")
    hidden_state = residual.astype(jnp.float32) + attended_sum
    model_width = w_gate.shape[1]
    row_count = steps_count * request_count
    whole_state, whole_gain = (
        lax.all_gather(hidden_state, "seq", axis=2, tiled=True),
        lax.all_gather(norm_gain, "seq", axis=0, tiled=True),
    )
    mean_square = jnp.mean(whole_state * whole_state, -1, keepdims=True)
    normed = (
        (whole_state * lax.rsqrt(mean_square + epsilon) * whole_gain)
        .astype(jnp.bfloat16)
        .reshape(row_count, model_width)
    )
    gate_sum = contract(normed, w_gate)
    up_sum = contract(normed, w_up)
    activation = (jax.nn.silu(gate_sum) * up_sum).astype(jnp.bfloat16)
    own_rows = model_width // (shard_count * head_count)
    mlp_rows = lax.psum_scatter(
        lax.dot_general(
            w_down, activation, (((0,), (1,)), ((), ())), preferred_element_type=jnp.float32
        ),
        ("seq", "head"),
        scatter_dimension=0,
        tiled=True,
    )
    own_columns = lax.dynamic_slice_in_dim(hidden_state, head_index * own_rows, own_rows, 2)
    result = own_columns + mlp_rows.T.reshape(steps_count, request_count, own_rows)
    return result.astype(jnp.bfloat16)


def solution(mesh):
    in_specs = (
        P(),
        P(),
        P(),
        P("seq", None, "head", None),
        P(None, "seq", "head", None),
        P(None, "seq", "head", None),
        P(None, None, "seq"),
        P("seq"),
        P("head", None, "seq"),
        P(("seq", "head"), None),
        P(("seq", "head"), None),
        P(("seq", "head"), None),
    )
    out_specs = P(None, None, ("seq", "head"))
    return jax.shard_map(shards, mesh=mesh, in_specs=in_specs, out_specs=out_specs, check_vma=False)
```

profile of v0, /device:TPU:1, one launch (start us, length us, event | category | flops | bytes accessed | tf_op | source)
XLA Modules:
  0.0 1734.5 jit_solution(17662751750708499638)
XLA Ops:
  6.5 0.8 fusion.37
  7.4 0.1 copy.21
  7.5 0.1 reduce-window.9
  7.5 0.1 reduce.8
  7.6 0.7 fusion.36
  8.3 0.7 compare_select_fusion.2
  9.0 0.7 gather_fusion
  9.7 0.1 compare_select_fusion.1
  9.8 0.1 copy.23
  9.9 0.1 copy.24
  9.9 0.1 reshape.458
  10.0 2.3 gather_fusion.1
  12.4 0.1 min.29
  12.5 0.1 reshape.466
  12.6 10.0 gather_fusion.2
  22.6 12.3 all-to-all-start
  34.9 0.6 dynamic_slice.6
  37.5 0.6 dynamic-slice.5
  40.0 0.7 dynamic-slice.4
  40.7 0.7 and_select_fusion.1
  41.4 0.1 add_multiply_fusion
  41.4 0.1 copy.22
  41.5 0.7 add_compare_fusion
  42.2 0.1 lt.80
  42.3 0.1 iota_compare_fusion
  42.4 0.2 fusion.29
  42.6 179.8 %all-to-all-done = bf16[1,32,8,64,256]{4,3,2,0,1:T(8,128)(2,1)} async-done(((bf16[1,32,8,64,256]{4,3,2,0,1:T(8,128)(2,1)}), bf16[1,32,8,64,256]{4,3,2,0,1:T(8,128)(2,1)}, u32[]{:S(2)}, u32[]{:S(2)}) %all-to-all-start) | async-done | bytes 8388640 | tf_op jit(solution)/shard_map/all_to_all | solution.py:67
  222.4 3.5 fusion.28
  225.9 0.2 fusion.24
  226.1 0.4 convert_reduce_fusion
  226.5 3.0 fusion.6
  229.5 40.2 %all_gather.9 = bf16[2,32,1024]{2,0,1:T(2,128)(2,1)S(1)} all-gather(bf16[2,1,1024]{2,0,1:T(2,128)(2,1)S(1)} %reshape_transpose.3), channel_id=1, replica_groups=mesh['seq'=32,'head'=8] {'seq'}, dimensions={1}, use_global_device_ids=true | all-gather | bytes 135168 | tf_op jit(solution)/shard_map/all_gather | solution.py:108
  269.7 2.2 fusion.8
  271.9 0.0 all-gather.3.cloned.1.call-start
  272.0 72.4 %all-reduce.2.cloned.1.call-done = f32[2,32,512]{2,1,0:T(8,128)} async-done(((f32[2,32,512]{2,1,0:T(8,128)}), f32[2,32,512]{2,1,0:T(8,128)}) %all-reduce.2.cloned.1.call-update) | async-done | bytes 131088 | tf_op jit(solution)/shard_map/psum | solution.py:112
  344.4 1.6 convert_add_fusion
  346.1 38.9 %all-gather = f32[32,1,512]{2,1,0:T(1,128)S(1)} all-gather(f32[1,1,512]{2,1,0:T(1,128)S(1)} %bitcast.83), channel_id=1, replica_groups=mesh['seq'=32,'head'=8] {'seq'}, dimensions={0}, use_global_device_ids=true | all-gather | bytes 67584 | tf_op jit(solution)/shard_map/all_gather | solution.py:118
  384.9 42.8 %all-gather.3.cloned.1.call-done = f32[2,32,16384]{2,1,0:T(8,128)} async-done(((f32[2,32,512]{2,1,0:T(8,128)}), f32[2,32,16384]{2,1,0:T(8,128)}) %all-gather.3.cloned.1.call-update) | async-done | bytes 4194320 | tf_op jit(solution)/shard_map/all_gather | solution.py:117
  427.7 2.8 multiply_reduce_fusion
  430.4 0.7 copy-done.3
  431.1 0.5 multiply_convert_fusion
  431.6 1.3 copy-done.2
  432.9 1.3 fusion.30
  434.3 7.3 convolution_bitcast_fusion
  441.6 6.9 copy.26
  448.5 1277.1 %reduce-scatter.4.cloned.1.call-done = f32[64,64]{1,0:T(8,128)} async-done(((f32[16384,64]{1,0:T(8,128)}), f32[64,64]{1,0:T(8,128)}) %reduce-scatter.4.cloned.1.call-update) | async-done | bytes 16400
  1725.7 0.8 copy.27
  1726.5 1.5 add_convert_fusion
  (40 shorter events, 0.3 us)
Async XLA Ops:
  6.5 427.7 %copy-start = (bf16[104,16384]{1,0:T(8,128)(2,1)S(1)}, bf16[104,16384]{1,0:T(8,128)(2,1)}, u32[]{:S(2)}) copy-start(bf16[104,16384]{1,0:T(8,128)(2,1)} %param.23) | copy-start | bytes 10223620
  6.5 3.5 copy-start.1
  22.6 12.4 copy-start.9
  22.6 14.9 copy-start.10
  22.6 19.8 %copy-start.7 = (bf16[3,1,1,256]{3,0,2,1:T(4,128)(2,1)S(1)}, bf16[3,1,1,256]{3,0,2,1:T(4,128)(2,1)}, u32[]{:S(2)}) copy-start(bf16[3,1,1,256]{3,0,2,1:T(4,128)(2,1)} %param.16) | copy-start | bytes 4612
  22.6 19.8 %copy-start.8 = (bf16[2,1,1,1024]{3,0,2,1:T(2,128)(2,1)S(1)}, bf16[2,1,1,1024]{3,0,2,1:T(2,128)(2,1)}, u32[]{:S(2)}) copy-start(bf16[2,1,1,1024]{3,0,2,1:T(2,128)(2,1)} %param.17) | copy-start | bytes 12292
  22.6 199.8 %all-to-all-start = ((bf16[1,32,8,64,256]{4,3,2,0,1:T(8,128)(2,1)}), bf16[1,32,8,64,256]{4,3,2,0,1:T(8,128)(2,1)}, u32[]{:S(2)}, u32[]{:S(2)}) async-start(bf16[1,32,8,64,256]{4,3,2,0,1:T(8,128)(2,1)} %bitcast.78), calls=%async_computation | async-start | bytes 16777216 | tf_op jit(solution)/shard_map/all_to_all | solution.py:67
  34.9 309.5 %all-reduce.2.cloned.1.call-start = ((), (), s32[]{:S(2)}) async-start(), calls=%async_computation.2 | async-start | bytes 262144 | tf_op jit(solution)/shard_map/psum | solution.py:112
  226.5 117.9 %copy-start.5 = (bf16[2,32,512]{2,1,0:T(8,128)(2,1)S(1)}, bf16[2,32,512]{2,1,0:T(8,128)(2,1)}, u32[]{:S(2)}) copy-start(bf16[2,32,512]{2,1,0:T(8,128)(2,1)} %param.18) | copy-start | bytes 196612
  226.5 119.6 %copy-start.6 = (f32[512]{0:T(512)S(1)}, f32[512]{0:T(512)}, u32[]{:S(2)}) copy-start(f32[512]{0:T(512)} %param.19) | copy-start | bytes 6148
  271.9 155.7 %all-gather.3.cloned.1.call-start = ((), (), s32[]{:S(2)}) async-start(), calls=%async_computation.3 | async-start | bytes 4325376 | tf_op jit(solution)/shard_map/all_gather | solution.py:117
  346.0 1379.7 %reduce-scatter.4.cloned.1.call-start = ((), (), s32[]{:S(2)}) async-start(), calls=%async_computation.4 | async-start | bytes 8421376
  427.7 3.4 copy-start.3
  430.4 2.5 copy-start.4
  431.6 1.4 copy-start.2
Sparse Core Ops, SparseCore 0:
  272.0 72.3 all-reduce.1
  347.3 80.3 all-gather.2
  448.7 1276.9 reduce-scatter.3
where the time goes:
time: 1740 us; the launch traced here: 1730 us
  waiting for transfers between devices  1570 us (90%)
  blocking collectives  79.1 us (5%)
  local copies, waits for them, and re-layouts  25.3 us (1%)
  matrix products  17.6 us (1%)
    unnamed x4, waiting for transfers between devices  1280 us
    all_to_all x1, waiting for transfers between devices, shards(): lax.all_to_all(outgoing, 'seq', split_axis=1, concat_axis=1, tiled=True)  180 us
    psum x1, waiting for transfers between devices, shards(): attended_sum = lax.psum(head_part, 'head')  72.4 us
    all_gather x1, waiting for transfers between devices, shards(): lax.all_gather(hidden_state, 'seq', axis=2, tiled=True)  42.8 us
    all_gather x1, blocking collectives, shards(): lax.all_gather(attended, 'seq', axis=1, tiled=True)  40.2 us
    all_gather x1, blocking collectives, shards(): lax.all_gather(norm_gain, 'seq', axis=0, tiled=True)  38.9 us
  transfers between devices with their start and end apart: 4, of which 4 were waited for; matrix products, arithmetic and copies ran while one was open for 0% of the time, Pallas kernels for 0%

commit v1 on v0

v1 whole, which is shorter than its diff:
```python
import math

import jax
import jax.numpy as jnp
from jax import lax
from jax.experimental import pallas as pl
from jax.experimental.pallas import tpu as pltpu
from jax.sharding import PartitionSpec as P

EPSILON = 1e-05
NZ, NY, NX, NC = 8, 4, 4, 2
NS, NH = NZ * NY, NX * NC
HD = 128
PAGE = 64
ROWS = 16
TOKENS = 4096
CHUNK = 256
FAR = 131072.0
F32, BF16 = jnp.float32, jnp.bfloat16
NT = (((1,), (1,)), ((), ()))
EXP_SCALE = math.log2(math.e) / math.sqrt(HD)


def iota(shape, dim):
    return lax.broadcasted_iota(jnp.int32, shape, dim)


def stat_tile(total):
    high = total.astype(BF16).astype(F32)
    row = iota((16, HD), 0)
    tile = jnp.where(row == 0, high, jnp.where(row == 1, total - high, 0.0))
    return tile.astype(BF16)


def kernel(
    lengths, slot_request, table, new_kv, queries, residual, gain,
    kv_hbm, wo_hbm, wg_hbm, wu_hbm, wd_hbm,
    out,
    kv, bias, wo, wg, wu, wd,
    qall, hot, codes, scores, peak, acc,
    ps, pr, ag, af, hp, hr, hid,
    zb, x1, y2, y1, x2, py1, px2,
    o1, o2, sb, rb, s1, r1, s2, rx2,
    t1f, t1b, rt1, t2f, t2b, rt2, us, ur,
    load_sem, snd, rcv, y_sem, x_sem, rb_sem,
):
    s = lax.axis_index("seq")
    h = lax.axis_index("head")
    z, y = s // NY, s % NY
    x, c = h // NC, h % NC
    partner = (s, x * NC + 1 - c)

    def at_y(other):
        return (z * NY + other, h)

    def at_x(other):
        return (s, other * NC + c)

    def send(src, dst, send_sem, recv_sem, device):
        pltpu.make_async_remote_copy(
            src_ref=src,
            dst_ref=dst,
            send_sem=send_sem,
            recv_sem=recv_sem,
            device_id=device,
            device_id_type=pl.DeviceIdType.MESH,
        ).start()

    def settle(like, sem):
        pltpu.make_async_copy(like, like, sem).wait()

    loads = [
        pltpu.make_async_copy(src, dst, load_sem.at[n])
        for n, (src, dst) in enumerate(
            ((kv_hbm, kv), (wo_hbm, wo), (wg_hbm, wg), (wu_hbm, wu), (wd_hbm, wd))
        )
    ]
    for load in loads:
        load.start()

    barrier = pltpu.get_barrier_semaphore()

    def greet(device):
        pl.semaphore_signal(barrier, inc=1, device_id=device, device_id_type=pl.DeviceIdType.MESH)

    @pl.loop(1, NS)
    def _(d):
        greet(((s + d) % NS, h))

    @pl.loop(1, NH)
    def _(d):
        greet((s, (h + d) % NH))

    @pl.loop(1, NZ)
    def _(d):
        greet((((z + d) % NZ) * NY + y, x * NC + 1 - c))

    row = iota((NS, HD), 0)
    length = jnp.zeros((NS, HD), jnp.int32)
    slot = jnp.zeros((NS, HD), jnp.int32)
    for r in range(NS):
        length = jnp.where(row == r, lengths[r], length)
        slot = jnp.where(row == slot_request[r], r, slot)
    halves = []
    for half in range(2):
        page = iota((NS, HD), 1) + half * HD
        filled = jnp.clip(length - page * PAGE, 0, PAGE)
        local = jnp.where(filled > 0, table[:, half * HD : (half + 1) * HD] - s * PAGE, -1)
        halves.append((local, (slot * HD + filled).astype(F32)))

    def find(p, carry):
        hits = [jnp.where(local == p, code, 0.0) for local, code in halves]
        codes[pl.ds(p, 1), :] = jnp.sum(hits[0] + hits[1], axis=0, keepdims=True)
        return carry

    lax.fori_loop(0, PAGE, find, 0)
    code = jnp.sum(codes[...], axis=1, keepdims=True)
    codes[...] = jnp.broadcast_to(code, (PAGE, HD))

    def cover(p, carry):
        both = codes[pl.ds(p, 1), :].astype(jnp.int32)
        mine = (iota((PAGE, HD), 1) == both // HD) & (iota((PAGE, HD), 0) < both % HD)
        bias[pl.ds(pl.multiple_of(p * PAGE, PAGE), PAGE), :] = jnp.where(mine, 0.0, -FAR).astype(BF16)
        return carry

    lax.fori_loop(0, PAGE, cover, 0)
    hot[...] = jnp.where(iota((NS * ROWS, HD), 0) // ROWS == iota((NS * ROWS, HD), 1), 1.0, 0.0).astype(BF16)

    wide = queries[...].astype(F32)
    own_query = jnp.concatenate(
        [wide[t : t + 1, g * HD : (g + 1) * HD] for t in range(2) for g in range(8)], axis=0
    )
    qall[s] = own_query.astype(BF16)

    pl.semaphore_wait(barrier, (NS - 1) + (NH - 1) + (NZ - 1))

    @pl.loop(1, NS)
    def _(d):
        send(qall.at[s], qall.at[s], snd.at[0], rcv.at[0], ((s + d) % NS, h))

    loads[0].wait()
    settle(qall.at[pl.ds(0, NS - 1)], rcv.at[0])

    aug_query = jnp.concatenate([qall[...].reshape(NS * ROWS, HD), hot[...]], axis=1)
    peak[...] = jnp.full((NS * ROWS, HD), -4.0 * FAR, F32)

    def score(k, carry):
        tokens = pl.ds(pl.multiple_of(k * CHUNK, CHUNK), CHUNK)
        aug_key = jnp.concatenate([kv[tokens, :HD], bias[tokens, :]], axis=1)
        raw = lax.dot_general(aug_query, aug_key, NT, preferred_element_type=F32)
        scores[:, tokens] = raw
        peak[...] = jnp.maximum(peak[...], jnp.maximum(raw[:, :HD], raw[:, HD:]))
        return carry

    lax.fori_loop(0, TOKENS // CHUNK, score, 0)
    top = jnp.max(peak[...], axis=1, keepdims=True).astype(BF16).astype(F32)
    peak[...] = jnp.broadcast_to(top, (NS * ROWS, HD))
    acc[...] = jnp.zeros((NS * ROWS, 2 * HD), F32)

    def mix(k, carry):
        tokens = pl.ds(pl.multiple_of(k * CHUNK, CHUNK), CHUNK)
        aug_value = jnp.concatenate([kv[tokens, HD:], jnp.ones((CHUNK, HD), BF16)], axis=1)
        base = jnp.concatenate([peak[...], peak[...]], axis=1)
        weights = jnp.exp2((scores[:, tokens] - base) * EXP_SCALE).astype(BF16)
        acc[...] += jnp.dot(weights, aug_value, preferred_element_type=F32)
        return carry

    lax.fori_loop(0, TOKENS // CHUNK, mix, 0)
    total = acc[:, HD:]
    high = total.astype(BF16).astype(F32)
    lane = iota((NS * ROWS, HD), 1)
    stats = jnp.where(lane == 0, peak[...], jnp.where(lane == 1, high, total - high))
    ps[:, :ROWS, :] = acc[:, :HD].astype(BF16).reshape(NS, ROWS, HD)
    ps[:, ROWS:, :] = stats.astype(BF16).reshape(NS, ROWS, HD)
    pr[s] = ps[s]

    @pl.loop(1, NS)
    def _(d):
        other = (s + d) % NS
        send(ps.at[other], pr.at[s], snd.at[1], rcv.at[1], (other, h))

    fresh = new_kv[...].astype(F32)
    late = iota((ROWS, 1), 0) >= ROWS // 2
    rounded_query = own_query.astype(BF16).astype(F32)
    fresh_scores = []
    for e in range(3):
        raw = jnp.sum(rounded_query * fresh[e : e + 1, :HD], axis=1, keepdims=True)
        fresh_scores.append(jnp.where(late, raw, -FAR) if e == 2 else raw)
    settle(pr.at[pl.ds(0, NS - 1)], rcv.at[1])
    stats = pr[:, ROWS:, :].astype(F32)
    tops = stats[:, :, 0:1]
    top = jnp.max(tops, axis=0)
    for raw in fresh_scores:
        top = jnp.maximum(top, raw)
    factor = jnp.exp2((tops - top[None]) * EXP_SCALE)
    total = jnp.sum(factor * (stats[:, :, 1:2] + stats[:, :, 2:3]), axis=0)
    mixed = jnp.sum(factor * pr[:, :ROWS, :].astype(F32), axis=0)
    for e, raw in enumerate(fresh_scores):
        weight = jnp.exp2((raw - top) * EXP_SCALE).astype(BF16).astype(F32)
        total = total + weight
        mixed = mixed + weight * fresh[e : e + 1, HD:]
    ag[s] = (mixed / total).astype(BF16)

    @pl.loop(1, NS)
    def _(d):
        send(ag.at[s], ag.at[s], snd.at[2], rcv.at[2], ((s + d) % NS, h))

    loads[1].wait()
    settle(ag.at[pl.ds(0, NS - 1)], rcv.at[2])

    af[...] = ag[...].reshape(NS * ROWS, HD).astype(F32)
    attended = jnp.concatenate(
        [
            jnp.concatenate([af[pl.ds(t * 8 + g, NS, stride=ROWS), :] for g in range(8)], axis=1)
            for t in range(2)
        ],
        axis=0,
    ).astype(BF16)
    part = jnp.dot(attended, wo[...], preferred_element_type=F32)
    for xx in range(NX):
        for cc in range(NC):
            hp[xx * NC + cc] = part[cc * NS : (cc + 1) * NS, xx * HD : (xx + 1) * HD]
    hr[h] = hp[h]

    @pl.loop(1, NH)
    def _(d):
        other = (h + d) % NH
        send(hp.at[other], hr.at[h], snd.at[3], rcv.at[3], (s, other))

    columns = pl.ds(pl.multiple_of(x * HD, HD), HD)
    settle(hr.at[pl.ds(0, NH - 1)], rcv.at[3])
    hidden = residual[c, :, columns].astype(F32) + jnp.sum(hr[...], axis=0)
    hid[c] = hidden
    square = jnp.sum(hidden * hidden, axis=1, keepdims=True)
    spread = jnp.where(iota((NS, HD), 0) == iota((NS, HD), 1), square, 0.0)
    zb[z, 0:32] = (hidden * gain[:, columns]).astype(BF16)
    zb[z, 32:48] = stat_tile(jnp.sum(spread, axis=0, keepdims=True))

    @pl.loop(1, NZ)
    def _(d):
        send(zb.at[z], zb.at[z], snd.at[4], rcv.at[4], (((z + d) % NZ) * NY + y, h))

    send(hid.at[c], hid.at[c], snd.at[5], rcv.at[5], partner)
    settle(zb.at[pl.ds(0, NZ - 1)], rcv.at[4])
    x1[x, 0:128] = zb[:, 0:16, :].reshape(128, HD)
    stats = jnp.sum(zb[:, 32:48, :].astype(F32), axis=0)
    x1[x, 128:144] = stat_tile(stats[0:1] + stats[1:2])
    y2[y] = zb[:, 16:32, :].reshape(128, HD)
    for d in range(1, 4):
        send(x1.at[x], x1.at[x], snd.at[6], rcv.at[6], at_x((x + d) % NX))
        send(y2.at[y], y2.at[y], snd.at[7], rcv.at[7], at_y((y + d) % NY))
    settle(x1.at[pl.ds(0, 3)], rcv.at[6])
    for xx in range(NX):
        y1[y, xx * 128 : (xx + 1) * 128] = x1[xx, 0:128]
    stats = jnp.sum(x1[:, 128:144, :].astype(F32), axis=0)
    y1[y, 512:528] = stat_tile(stats[0:1] + stats[1:2])
    for d in range(1, 4):
        send(y1.at[y], y1.at[y], snd.at[8], y_sem.at[d - 1], at_y((y + d) % NY))
    send(y1.at[y], py1.at[y], snd.at[10], rcv.at[8], partner)
    settle(y2.at[pl.ds(0, 3)], rcv.at[7])
    for yy in range(NY):
        x2[x, yy * 128 : (yy + 1) * 128] = y2[yy]
    for d in range(1, 4):
        send(x2.at[x], x2.at[x], snd.at[9], x_sem.at[d - 1], at_x((x + d) % NX))
    send(x2.at[x], px2.at[x], snd.at[11], rcv.at[9], partner)
    for d in range(1, 4):
        origin = (y + NY - d) % NY
        settle(y1.at[origin], y_sem.at[d - 1])
        send(y1.at[origin], py1.at[origin], snd.at[10], rcv.at[8], partner)
        origin = (x + NX - d) % NX
        settle(x2.at[origin], x_sem.at[d - 1])
        send(x2.at[origin], px2.at[origin], snd.at[11], rcv.at[9], partner)
    loads[2].wait()
    loads[3].wait()
    settle(py1, rcv.at[8])
    settle(px2, rcv.at[9])

    def gate_up(n, carry):
        gate, up = carry
        yy, xp = n // 2, n % 2
        for zz in range(NZ):
            pieces = []
            for first, second in ((y1, x2), (py1, px2)):
                pieces.append(
                    jnp.concatenate(
                        [
                            first[yy, pl.ds(pl.multiple_of((xp * 2 + e) * 128 + zz * 16, 16), 16), :]
                            for e in range(2)
                        ],
                        axis=1,
                    )
                )
                pieces.append(
                    jnp.concatenate(
                        [
                            second[xp * 2 + e, pl.ds(pl.multiple_of(yy * 128 + zz * 16, 16), 16), :]
                            for e in range(2)
                        ],
                        axis=1,
                    )
                )
            stream = jnp.concatenate(pieces, axis=0)
            where = pl.ds(pl.multiple_of(zz * 2048 + yy * 512 + xp * 256, 256), 256)
            gate = gate + lax.dot_general(stream, wg[:, where], NT, preferred_element_type=F32)
            up = up + lax.dot_general(stream, wu[:, where], NT, preferred_element_type=F32)
        return gate, up

    zero = jnp.zeros((64, 104), F32)
    gate, up = lax.fori_loop(0, 8, gate_up, (zero, zero))
    own_stats = jnp.sum(y1[:, 512:528, :].astype(F32), axis=0)
    other_stats = jnp.sum(py1[:, 512:528, :].astype(F32), axis=0)
    square = jnp.concatenate(
        [
            jnp.sum(
                jnp.where(iota((NS, HD), 0) == iota((NS, HD), 1), tile[0:1] + tile[1:2], 0.0),
                axis=1,
                keepdims=True,
            )
            for tile in (own_stats, other_stats)
        ],
        axis=0,
    )
    scale = lax.rsqrt(square * (1.0 / 16384.0) + EPSILON)
    gate = gate * scale
    up = up * scale
    activation = (gate / (1.0 + jnp.exp(-gate)) * up).astype(BF16)

    loads[4].wait()

    def down(k):
        yy = (y + k + 1) % NY

        def body(xp, carry):
            for zz in range(NZ):
                where = pl.ds(pl.multiple_of(zz * 2048 + yy * 512 + xp * 256, 256), 256)
                block = jnp.dot(activation, wd[:, where], preferred_element_type=F32)
                for e in range(2):
                    piece = block[:, e * HD : (e + 1) * HD]
                    at = pl.multiple_of((xp * 2 + e) * 128 + zz * 16, 16)
                    o1[k, pl.ds(at, 16), :] = piece[0:16]
                    o2[k, pl.ds(at, 16), :] = piece[16:32]
                    sb[k, pl.ds(at, 16), :] = piece[32:48].astype(BF16)
                    sb[k, pl.ds(at + 512, 16), :] = piece[48:64].astype(BF16)
            return carry

        lax.fori_loop(0, 2, body, 0)
        send(sb.at[k], rb.at[k], snd.at[12], rb_sem.at[k], partner)

    def finish(k):
        yy = (y + k + 1) % NY
        settle(rb.at[k], rb_sem.at[k])
        first = o1[k] + rb[k, 0:512].astype(F32)
        if k < 3:
            s1[k] = first.astype(BF16)
            send(s1.at[k], r1.at[k], snd.at[13], rcv.at[10], at_y(yy))
        else:
            o1[k] = first
        second = o2[k] + rb[k, 512:1024].astype(F32)
        o2[k] = second
        for xx in range(NX):
            s2[xx, pl.ds(pl.multiple_of(yy * 128, 128), 128), :] = second[xx * 128 : (xx + 1) * 128].astype(BF16)

    for k in range(4):
        down(k)
        if k > 0:
            finish(k - 1)
    finish(3)
    for j in range(3):
        other = (x + j + 1) % NX
        send(s2.at[other], rx2.at[j], snd.at[14], rcv.at[11], at_x(other))

    settle(r1, rcv.at[10])
    whole = o1[3]
    for j in range(3):
        whole = whole + r1[j].astype(F32)
    t1f[...] = whole.reshape(NX, 128, HD)
    t1b[...] = whole.reshape(NX, 128, HD).astype(BF16)
    for j in range(3):
        other = (x + j + 1) % NX
        send(t1b.at[other], rt1.at[j], snd.at[15], rcv.at[12], at_x(other))

    settle(rx2, rcv.at[11])
    for k in range(4):
        yy = (y + k + 1) % NY
        rows = pl.ds(pl.multiple_of(yy * 128, 128), 128)
        whole = o2[k, pl.ds(pl.multiple_of(x * 128, 128), 128), :]
        for j in range(3):
            whole = whole + rx2[j, rows, :].astype(F32)
        if k < 3:
            t2b[k] = whole.astype(BF16)
            send(t2b.at[k], rt2.at[k], snd.at[16], rcv.at[13], at_y(yy))
        else:
            t2f[...] = whole

    settle(rt1, rcv.at[12])
    whole = t1f[x]
    for j in range(3):
        whole = whole + rt1[j].astype(F32)
    us[:, 0:16, :] = whole.reshape(NZ, 16, HD).astype(BF16)
    settle(rt2, rcv.at[13])
    whole = t2f[...]
    for j in range(3):
        whole = whole + rt2[j].astype(F32)
    us[:, 16:32, :] = whole.reshape(NZ, 16, HD).astype(BF16)
    ur[c * NZ + z] = us[z]

    @pl.loop(1, NZ)
    def _(d):
        other = (z + d) % NZ
        send(us.at[other], ur.at[c * NZ + z], snd.at[17], rcv.at[14], (other * NY + y, h))
        send(us.at[other], ur.at[c * NZ + z], snd.at[17], rcv.at[14], (other * NY + y, x * NC + 1 - c))

    send(us.at[z], ur.at[c * NZ + z], snd.at[17], rcv.at[14], partner)
    settle(hid.at[0], rcv.at[5])
    settle(ur.at[pl.ds(0, 15)], rcv.at[14])
    for t in range(2):
        result = hid[t] + jnp.sum(ur[t * NZ : (t + 1) * NZ].astype(F32), axis=0)
        out[t] = jnp.where(c == 0, result[:, :64], result[:, 64:]).astype(BF16)

    for like, n in (
        (qall.at[pl.ds(0, NS - 1)], 0),
        (ps.at[pl.ds(0, NS - 1)], 1),
        (ag.at[pl.ds(0, NS - 1)], 2),
        (hp.at[pl.ds(0, NH - 1)], 3),
        (zb.at[pl.ds(0, NZ - 1)], 4),
        (hid.at[0], 5),
        (x1.at[pl.ds(0, 3)], 6),
        (y2.at[pl.ds(0, 3)], 7),
        (y1.at[pl.ds(0, 3)], 8),
        (x2.at[pl.ds(0, 3)], 9),
        (y1, 10),
        (x2, 11),
        (sb, 12),
        (s1, 13),
        (s2.at[pl.ds(0, 3)], 14),
        (rt1, 15),
        (rt2, 16),
        (ur.at[pl.ds(0, 15)], 17),
    ):
        settle(like, snd.at[n])


def shards(
    lengths,
    block_table,
    slot_request,
    kv_pool,
    new_kv,
    queries,
    residual,
    norm_gain,
    w_out,
    w_gate,
    w_up,
    w_down,
):
    vmem = pl.BlockSpec(memory_space=pltpu.VMEM)
    smem = pl.BlockSpec(memory_space=pltpu.SMEM)
    anywhere = pl.BlockSpec(memory_space=pl.ANY)
    scratch = [
        ((TOKENS, 256), BF16),
        ((TOKENS, HD), BF16),
        ((1024, 512), BF16),
        ((104, 16384), BF16),
        ((104, 16384), BF16),
        ((104, 16384), BF16),
        ((NS, ROWS, HD), BF16),
        ((NS * ROWS, HD), BF16),
        ((PAGE, HD), F32),
        ((NS * ROWS, TOKENS), F32),
        ((NS * ROWS, HD), F32),
        ((NS * ROWS, 256), F32),
        ((NS, 32, HD), BF16),
        ((NS, 32, HD), BF16),
        ((NS, ROWS, HD), BF16),
        ((NS * ROWS, HD), F32),
        ((NH, 32, HD), F32),
        ((NH, 32, HD), F32),
        ((2, 32, HD), F32),
        ((NZ, 48, HD), BF16),
        ((NX, 144, HD), BF16),
        ((NY, 128, HD), BF16),
        ((NY, 528, HD), BF16),
        ((NX, 512, HD), BF16),
        ((NY, 528, HD), BF16),
        ((NX, 512, HD), BF16),
        ((4, 512, HD), F32),
        ((4, 512, HD), F32),
        ((4, 1024, HD), BF16),
        ((4, 1024, HD), BF16),
        ((3, 512, HD), BF16),
        ((3, 512, HD), BF16),
        ((4, 512, HD), BF16),
        ((3, 512, HD), BF16),
        ((4, 128, HD), F32),
        ((4, 128, HD), BF16),
        ((3, 128, HD), BF16),
        ((128, HD), F32),
        ((3, 128, HD), BF16),
        ((3, 128, HD), BF16),
        ((NZ, 32, HD), BF16),
        ((2 * NZ, 32, HD), BF16),
    ]
    return pl.pallas_call(
        kernel,
        out_shape=jax.ShapeDtypeStruct((2, NS, 64), BF16),
        in_specs=[smem, smem] + [vmem] * 5 + [anywhere] * 5,
        out_specs=vmem,
        scratch_shapes=[pltpu.VMEM(shape, kind) for shape, kind in scratch]
        + [pltpu.SemaphoreType.DMA((n,)) for n in (5, 18, 15, 3, 3, 4)],
        compiler_params=pltpu.CompilerParams(
            collective_id=0, has_side_effects=True, vmem_limit_bytes=56 * 1024 * 1024
        ),
    )(
        lengths,
        slot_request,
        block_table,
        new_kv.reshape(3, 256),
        queries.reshape(2, 1024),
        residual,
        norm_gain.reshape(1, 512),
        kv_pool.reshape(TOKENS, 256),
        w_out.reshape(1024, 512),
        w_gate,
        w_up,
        w_down,
    )


def solution(mesh):
    in_specs = (
        P(),
        P(),
        P(),
        P("seq", None, "head", None),
        P(None, "seq", "head", None),
        P(None, "seq", "head", None),
        P(None, None, "seq"),
        P("seq"),
        P("head", None, "seq"),
        P(("seq", "head"), None),
        P(("seq", "head"), None),
        P(("seq", "head"), None),
    )
    out_specs = P(None, None, ("seq", "head"))
    return jax.shard_map(shards, mesh=mesh, in_specs=in_specs, out_specs=out_specs, check_vma=False)
```

time: 1740 us -> 93.9 us (0.05)
  waiting for transfers between devices: 1570 us -> 0 us
  Pallas kernels: 0 us -> 92.3 us
  blocking collectives: 79.1 us -> 0 us
  local copies, waits for them, and re-layouts: 25.3 us -> 1.32 us
  matrix products: 17.6 us -> 0 us
    unnamed x4 -> x0, waiting for transfers between devices: 1280 us -> none
    all_to_all x1 -> x0, waiting for transfers between devices: 180 us -> none  [shards(): lax.all_to_all(outgoing, 'seq', split_axis=1, concat_axis=1, tiled=True)]
    pallas_call x0 -> x1, Pallas kernels: none -> 92.3 us  [shards(): pl.pallas_call(kernel, out_shape=jax.ShapeDtypeStruct((2, NS, 64), BF16),...]
    all_gather x2 -> x0, blocking collectives: 79.1 us -> none  [the longest x1 40.2 us: shards(): lax.all_gather(attended, 'seq', axis=1, tiled=True)]
    psum x1 -> x0, waiting for transfers between devices: 72.4 us -> none  [shards(): attended_sum = lax.psum(head_part, 'head')]
    all_gather x1 -> x0, waiting for transfers between devices: 42.8 us -> none  [shards(): lax.all_gather(hidden_state, 'seq', axis=2, tiled=True)]
    dot_general x7 -> x0, matrix products: 17.6 us -> none  [the longest x1 7.34 us: shards(): lax.dot_general(w_down, activation, (((0,), (1,)), ((), ())), preferred_e...]
  transfers between devices with their start and end apart: 4 -> 0, of which waited for: 4 -> 0; matrix products, arithmetic and copies ran while one was open for 0% -> 0% of each run, Pallas kernels for 0% -> 0%
where the time goes in v1:
time: 93.9 us; the launch traced here: 93.7 us
  Pallas kernels  92.3 us (98%)
  local copies, waits for them, and re-layouts  1.32 us (1%)
    pallas_call x1, Pallas kernels, shards(): pl.pallas_call(kernel, out_shape=jax.ShapeDtypeStruct((2, NS, 64), BF16),...  92.3 us

profile of v1, /device:TPU:1, one launch (start us, length us, event | category | flops | bytes accessed | tf_op | source)
XLA Modules:
  0.0 93.7 jit_solution(13228670013407005407)
XLA Ops:
  0.0 92.3 %shard_map.118 = bf16[2,32,64]{2,1,0:T(8,128)(2,1)} custom-call(s32[32]{0:T(128)} %lengths.1, s32[32]{0:T(128)} %slot_request.1, s32[32,256]{1,0:T(8,128)} %table.1, bf16[3,256]{1,0:T(4,128)(2,1)} %bitcast.8, bf16[2,1024]{1,0:T(2,128)(2,1)} %bitcast.7, bf16[2,32,512]{2,1,0:T(8,128)(2,1)} %residual.1, f32[1,512]{1,0:T(1,128)} %bitcast.9, ...), custom_call_target="tpu_custom_call" | custom-call | tf_op jit(solution)/shard_map/pallas_call | solution.py:504
  92.3 1.3 %copy.14 = bf16[2,32,64]{2,1,0:T(8,128)(2,1)} copy(bf16[2,32,64]{2,1,0:T(8,128)(2,1)} %shard_map.118) | data formatting | bytes 16384

commit v2 on v1

v2 whole, which is shorter than its diff:
```python
import functools
import math

import jax
import jax.numpy as jnp
from jax import lax
from jax.experimental import pallas as pl
from jax.experimental.pallas import tpu as pltpu
from jax.sharding import PartitionSpec as P

EPSILON = 1e-05
NZ, NY, NX, NC = 8, 4, 4, 2
NS, NH = NZ * NY, NX * NC
HD = 128
PAGE = 64
ROWS = 16
TOKENS = 4096
CHUNK = 512
FAR = 131072.0
F32, BF16 = jnp.float32, jnp.bfloat16
NT = (((1,), (1,)), ((), ()))
EXP_SCALE = math.log2(math.e) / math.sqrt(HD)


RING = (1, 3, 2)
AROUND = sorted(
    ((dz, dy) for dz in range(NZ) for dy in range(NY) if dz or dy),
    key=lambda d: -(min(d[0], NZ - d[0]) + min(d[1], NY - d[1])),
)


def iota(shape, dim):
    return lax.broadcasted_iota(jnp.int32, shape, dim)


def kernel(
    lengths, slot_request, table, new_kv, queries, residual, gain,
    kv_hbm, wo_hbm, wg_hbm, wu_hbm, wd_hbm,
    out,
    kv, bias, wo, wg, wu, wd,
    qall, hot, codes, scores, peak, acc,
    ps, pr, ss, sr, ag, af, hp, hr, hid,
    zb, sqz, sqx, sqy, sqp, ga, gb, pa, pb,
    o1, sb, rb, s1, r1, t1, s2, r2, us, ur,
    load_sem, snd, rcv, a2, b2, a3, b3, pa_sem, pb_sem, rb_sem, r1_sem,
):
    s = lax.axis_index("seq")
    h = lax.axis_index("head")
    z, y = s // NY, s % NY
    x, c = h // NC, h % NC
    partner = (s, x * NC + 1 - c)

    def shard(dz, dy):
        return ((z + dz) % NZ) * NY + (y + dy) % NY

    def at_y(other):
        return (z * NY + other, h)

    def at_x(other):
        return (s, other * NC + c)

    def send(src, dst, send_sem, recv_sem, device):
        pltpu.make_async_remote_copy(
            src_ref=src,
            dst_ref=dst,
            send_sem=send_sem,
            recv_sem=recv_sem,
            device_id=device,
            device_id_type=pl.DeviceIdType.MESH,
        ).start()

    def settle(like, sem):
        pltpu.make_async_copy(like, like, sem).wait()

    loads = [
        pltpu.make_async_copy(src, dst, load_sem.at[n])
        for n, (src, dst) in enumerate(
            ((kv_hbm, kv), (wo_hbm, wo), (wg_hbm, wg), (wu_hbm, wu), (wd_hbm, wd))
        )
    ]
    for load in loads:
        load.start()

    barrier = pltpu.get_barrier_semaphore()

    def greet(device):
        pl.semaphore_signal(barrier, inc=1, device_id=device, device_id_type=pl.DeviceIdType.MESH)

    for dz, dy in AROUND:
        greet((shard(dz, dy), h))

    @pl.loop(1, NH)
    def _(d):
        greet((s, (h + d) % NH))

    @pl.loop(1, NZ)
    def _(d):
        greet((((z + d) % NZ) * NY + y, x * NC + 1 - c))

    wide = queries[...].astype(F32)
    own_query = jnp.concatenate(
        [wide[t : t + 1, g * HD : (g + 1) * HD] for t in range(2) for g in range(8)], axis=0
    )
    qall[s] = own_query.astype(BF16)

    pl.semaphore_wait(barrier, (NS - 1) + (NH - 1) + (NZ - 1))

    for dz, dy in AROUND:
        send(qall.at[s], qall.at[s], snd.at[0], rcv.at[0], (shard(dz, dy), h))

    row = iota((NS, HD), 0)
    length = jnp.zeros((NS, HD), jnp.int32)
    slot = jnp.zeros((NS, HD), jnp.int32)
    for r in range(NS):
        length = jnp.where(row == r, lengths[r], length)
        slot = jnp.where(row == slot_request[r], r, slot)
    halves = []
    for half in range(2):
        page = iota((NS, HD), 1) + half * HD
        filled = jnp.clip(length - page * PAGE, 0, PAGE)
        local = jnp.where(filled > 0, table[:, half * HD : (half + 1) * HD] - s * PAGE, -1)
        halves.append((local, (slot * HD + filled).astype(F32)))

    def find(p, carry):
        hits = [jnp.where(local == p, code, 0.0) for local, code in halves]
        codes[pl.ds(p, 1), :] = jnp.sum(hits[0] + hits[1], axis=0, keepdims=True)
        return carry

    lax.fori_loop(0, PAGE, find, 0)
    code = jnp.sum(codes[...], axis=1, keepdims=True)
    codes[...] = jnp.broadcast_to(code, (PAGE, HD))

    def cover(p, carry):
        both = codes[pl.ds(p, 1), :].astype(jnp.int32)
        mine = (iota((PAGE, HD), 1) == both // HD) & (iota((PAGE, HD), 0) < both % HD)
        bias[pl.ds(pl.multiple_of(p * PAGE, PAGE), PAGE), :] = jnp.where(mine, 0.0, -FAR).astype(BF16)
        return carry

    lax.fori_loop(0, PAGE, cover, 0)
    hot[...] = jnp.where(iota((NS * ROWS, HD), 0) // ROWS == iota((NS * ROWS, HD), 1), 1.0, 0.0).astype(BF16)

    loads[0].wait()
    settle(qall.at[pl.ds(0, NS - 1)], rcv.at[0])

    aug_query = jnp.concatenate([qall[...].reshape(NS * ROWS, HD), hot[...]], axis=1)
    peak[...] = jnp.full((NS * ROWS, HD), -4.0 * FAR, F32)

    def score(k, carry):
        tokens = pl.ds(pl.multiple_of(k * CHUNK, CHUNK), CHUNK)
        aug_key = jnp.concatenate([kv[tokens, :HD], bias[tokens, :]], axis=1)
        raw = lax.dot_general(aug_query, aug_key, NT, preferred_element_type=F32)
        scores[:, tokens] = raw
        peak[...] = jnp.maximum(peak[...], functools.reduce(jnp.maximum, [raw[:, n : n + HD] for n in range(0, CHUNK, HD)]))
        return carry

    lax.fori_loop(0, TOKENS // CHUNK, score, 0, unroll=True)
    top = jnp.max(peak[...], axis=1, keepdims=True).astype(BF16).astype(F32)
    peak[...] = jnp.broadcast_to(top, (NS * ROWS, HD))
    acc[...] = jnp.zeros((NS * ROWS, 2 * HD), F32)

    def mix(k, carry):
        tokens = pl.ds(pl.multiple_of(k * CHUNK, CHUNK), CHUNK)
        aug_value = jnp.concatenate([kv[tokens, HD:], jnp.ones((CHUNK, HD), BF16)], axis=1)
        base = jnp.concatenate([peak[...]] * (CHUNK // HD), axis=1)
        weights = jnp.exp2((scores[:, tokens] - base) * EXP_SCALE).astype(BF16)
        acc[...] += jnp.dot(weights, aug_value, preferred_element_type=F32)
        return carry

    lax.fori_loop(0, TOKENS // CHUNK, mix, 0, unroll=True)
    acc_rows = acc[:, :HD].astype(BF16).reshape(NS, ROWS, HD)
    ps[...] = acc_rows
    cube = (NS, ROWS, HD)
    lane, line = iota(cube, 2), iota(cube, 1)
    stats = jnp.where(lane == line, peak[...].reshape(cube), 0.0)
    stats = jnp.where(lane == line + ROWS, acc[:, HD:].reshape(cube), stats)
    ss[...] = jnp.sum(stats, axis=1, keepdims=True)
    pr[s] = ps[s]
    sr[s] = ss[s]
    for dz, dy in AROUND:
        other = shard(dz, dy)
        send(ps.at[other], pr.at[s], snd.at[1], rcv.at[1], (other, h))
        send(ss.at[other], sr.at[s], snd.at[20], rcv.at[13], (other, h))

    fresh = new_kv[...].astype(F32)
    late = iota((ROWS, 1), 0) >= ROWS // 2
    rounded_query = own_query.astype(BF16).astype(F32)
    fresh_scores = []
    for e in range(3):
        raw = jnp.sum(rounded_query * fresh[e : e + 1, :HD], axis=1, keepdims=True)
        fresh_scores.append(jnp.where(late, raw, -FAR) if e == 2 else raw)
    settle(pr.at[pl.ds(0, NS - 1)], rcv.at[1])
    settle(sr.at[pl.ds(0, NS - 1)], rcv.at[13])
    stats = jnp.broadcast_to(sr[...], cube)
    tops = jnp.sum(jnp.where(lane == line, stats, 0.0), axis=2, keepdims=True)
    sums = jnp.sum(jnp.where(lane == line + ROWS, stats, 0.0), axis=2, keepdims=True)
    top = jnp.max(tops, axis=0)
    for raw in fresh_scores:
        top = jnp.maximum(top, raw)
    factor = jnp.exp2((tops - top[None]) * EXP_SCALE)
    total = jnp.sum(factor * sums, axis=0)
    mixed = jnp.sum(factor * pr[...].astype(F32), axis=0)
    for e, raw in enumerate(fresh_scores):
        weight = jnp.exp2((raw - top) * EXP_SCALE).astype(BF16).astype(F32)
        total = total + weight
        mixed = mixed + weight * fresh[e : e + 1, HD:]
    ag[s] = (mixed / total).astype(BF16)

    for dz, dy in AROUND:
        send(ag.at[s], ag.at[s], snd.at[2], rcv.at[2], (shard(dz, dy), h))

    loads[1].wait()
    settle(ag.at[pl.ds(0, NS - 1)], rcv.at[2])

    af[...] = ag[...].reshape(NS * ROWS, HD).astype(F32)
    attended = jnp.concatenate(
        [
            jnp.concatenate([af[pl.ds(t * 8 + g, NS, stride=ROWS), :] for g in range(8)], axis=1)
            for t in range(2)
        ],
        axis=0,
    ).astype(BF16)
    part = jnp.dot(attended, wo[...], preferred_element_type=F32)
    for xx in range(NX):
        for cc in range(NC):
            hp[xx * NC + cc] = part[cc * NS : (cc + 1) * NS, xx * HD : (xx + 1) * HD]
    hr[h] = hp[h]

    @pl.loop(1, NH)
    def _(d):
        other = (h + d) % NH
        send(hp.at[other], hr.at[h], snd.at[3], rcv.at[3], (s, other))

    columns = pl.ds(pl.multiple_of(x * HD, HD), HD)
    settle(hr.at[pl.ds(0, NH - 1)], rcv.at[3])
    hidden = residual[c, :, columns].astype(F32) + jnp.sum(hr[...], axis=0)
    hid[c] = hidden
    square = jnp.sum(hidden * hidden, axis=1, keepdims=True)
    zb[z] = (hidden * gain[:, columns]).astype(BF16)
    spread = jnp.where(iota((NS, HD), 0) == iota((NS, HD), 1), square, 0.0)
    sqz[z] = jnp.sum(spread, axis=0, keepdims=True)

    for d in (4, 3, 5, 2, 6, 1, 7):
        there = (((z + d) % NZ) * NY + y, h)
        send(zb.at[z], zb.at[z], snd.at[4], rcv.at[4], there)
        send(sqz.at[z], sqz.at[z], snd.at[5], rcv.at[5], there)
    send(hid.at[c], hid.at[c], snd.at[6], rcv.at[6], partner)
    settle(zb.at[pl.ds(0, NZ - 1)], rcv.at[4])

    ga[y, x] = zb[0:4].reshape(128, HD)
    gb[x, y] = zb[4:8].reshape(128, HD)

    def on_a(xx, n):
        for d in RING:
            send(ga.at[y, xx], ga.at[y, xx], snd.at[9], a3.at[n, d - 1], at_y((y + d) % NY))

    def on_b(yy, n):
        for d in RING:
            send(gb.at[x, yy], gb.at[x, yy], snd.at[10], b3.at[n, d - 1], at_x((x + d) % NX))

    def across(yy, xx, n):
        send(ga.at[yy, xx], pa.at[yy, xx], snd.at[11], pa_sem.at[n], partner)

    def across_b(xx, yy, n):
        send(gb.at[xx, yy], pb.at[xx, yy], snd.at[12], pb_sem.at[n], partner)

    for d in RING:
        send(ga.at[y, x], ga.at[y, x], snd.at[7], a2.at[d - 1], at_x((x + d) % NX))
        send(gb.at[x, y], gb.at[x, y], snd.at[8], b2.at[d - 1], at_y((y + d) % NY))
    on_a(x, 0)
    on_b(y, 0)
    across(y, x, 0)
    across_b(x, y, 0)
    settle(sqz.at[pl.ds(0, NZ - 1)], rcv.at[5])
    sqx[x] = jnp.sum(sqz[...], axis=0)
    for d in RING:
        send(sqx.at[x], sqx.at[x], snd.at[13], rcv.at[7], at_x((x + d) % NX))

    done = []
    done.append(("a", y, x, 0))
    done.append(("b", x, y, 0))
    for n, d in enumerate(RING):
        xx, yy = (x + NX - d) % NX, (y + NY - d) % NY
        settle(ga.at[y, xx], a2.at[d - 1])
        on_a(xx, n + 1)
        across(y, xx, n + 1)
        done.append(("a", y, xx, n + 1))
        settle(gb.at[x, yy], b2.at[d - 1])
        on_b(yy, n + 1)
        across_b(x, yy, n + 1)
        done.append(("b", x, yy, n + 1))
    settle(sqx.at[pl.ds(0, NX - 1)], rcv.at[7])
    sqy[y] = jnp.sum(sqx[...], axis=0)
    for d in RING:
        send(sqy.at[y], sqy.at[y], snd.at[14], rcv.at[8], at_y((y + d) % NY))

    loads[2].wait()
    loads[3].wait()
    gate = jnp.zeros((64, 104), F32)
    up = jnp.zeros((64, 104), F32)

    def multiply(item, sums):
        half, outer, inner, n = item
        if half == "a":
            settle(pa.at[outer, inner], pa_sem.at[n])
            own, other, yy, xx, first = ga, pa, outer, inner, 0
        else:
            settle(pb.at[outer, inner], pb_sem.at[n])
            own, other, yy, xx, first = gb, pb, inner, outer, 4
        stream = jnp.concatenate(
            [
                jnp.concatenate([ref[outer, inner, zz * 32 : (zz + 1) * 32] for zz in range(4)], axis=1)
                for ref in (own, other)
            ],
            axis=0,
        )
        where = [
            pl.ds(pl.multiple_of((first + zz) * 2048 + yy * 512 + xx * HD, HD), HD) for zz in range(4)
        ]
        return tuple(
            total
            + lax.dot_general(
                stream,
                jnp.concatenate([ref[:, w] for w in where], axis=1),
                NT,
                preferred_element_type=F32,
            )
            for total, ref in zip(sums, (wg, wu), strict=True)
        )

    sums = (gate, up)
    arrivals = []
    for n, k in enumerate((0,) + RING):
        for d in RING:
            arrivals.append(("a", (y + NY - d) % NY, (x + NX - k) % NX, n, d))
            arrivals.append(("b", (x + NX - d) % NX, (y + NY - k) % NY, n, d))
    for m, (half, outer, inner, n, d) in enumerate(arrivals):
        place = 4 + m // 2
        if half == "a":
            settle(ga.at[outer, inner], a3.at[n, d - 1])
            across(outer, inner, place)
        else:
            settle(gb.at[outer, inner], b3.at[n, d - 1])
            across_b(outer, inner, place)
        done.append((half, outer, inner, place))
        for _ in range(1 if m < len(arrivals) - 8 else 1):
            sums = multiply(done.pop(0), sums)
    for item in done:
        sums = multiply(item, sums)
    gate, up = sums
    settle(sqy.at[pl.ds(0, NY - 1)], rcv.at[8])
    sqp[0] = jnp.sum(sqy[...], axis=0)
    send(sqp.at[0], sqp.at[1], snd.at[15], rcv.at[9], partner)
    settle(sqp.at[0], rcv.at[9])
    square = jnp.concatenate(
        [
            jnp.sum(
                jnp.where(iota((NS, HD), 0) == iota((NS, HD), 1), sqp[n], 0.0), axis=1, keepdims=True
            )
            for n in range(2)
        ],
        axis=0,
    )
    scale = lax.rsqrt(square * (1.0 / 16384.0) + EPSILON)
    gate = gate * scale
    up = up * scale
    activation = (gate / (1.0 + jnp.exp(-gate)) * up).astype(BF16)

    loads[4].wait()
    turn = RING + (0,)
    spots = [[(y + b) % NY, (x + b) % NX] for b in turn]

    def groups(k):
        return [(spots[b][0], spots[k][1], 0) for b in range(4)] + [
            (spots[k][0], spots[b][1], 4) for b in range(4)
        ]

    def down(k):
        for m, (yy, xx, first) in enumerate(groups(k)):
            weight = jnp.concatenate(
                [
                    wd[:, pl.ds(pl.multiple_of((first + zz) * 2048 + yy * 512 + xx * HD, HD), HD)]
                    for zz in range(4)
                ],
                axis=1,
            )
            block = jnp.dot(activation, weight, preferred_element_type=F32)
            for zz in range(4):
                at = slice(m * 128 + zz * 32, m * 128 + (zz + 1) * 32)
                piece = block[:, zz * HD : (zz + 1) * HD]
                o1[k, at] = piece[0:32]
                sb[k, at] = piece[32:64].astype(BF16)
        send(sb.at[k], rb.at[k], snd.at[16], rb_sem.at[k], partner)

    def finish(k):
        settle(rb.at[k], rb_sem.at[k])
        for half in range(2):
            for b in range(4):
                at = slice((half * 4 + b) * 128, (half * 4 + b + 1) * 128)
                whole = o1[k, at] + rb[k, at].astype(F32)
                if b == 3:
                    t1[k, half] = whole
                else:
                    s1[k, half * 3 + b] = whole.astype(BF16)
                    there = at_x(spots[b][1]) if half else at_y(spots[b][0])
                    send(s1.at[k, half * 3 + b], r1.at[k, half * 3 + b], snd.at[17], r1_sem.at[k], there)

    def reduce_one(k):
        settle(r1.at[k], r1_sem.at[k])
        for half in range(2):
            whole = t1[k, half]
            for b in range(3):
                whole = whole + r1[k, half * 3 + b].astype(F32)
            if k == 3:
                t1[k, half] = whole
            else:
                s2[half, k] = whole.astype(BF16)
                there = at_y(spots[k][0]) if half else at_x(spots[k][1])
                send(s2.at[half, k], r2.at[half, k], snd.at[18], rcv.at[10 + half], there)

    for k in range(4):
        down(k)
        if k > 0:
            finish(k - 1)
    finish(3)
    for k in range(4):
        reduce_one(k)
    for half in range(2):
        settle(r2.at[half], rcv.at[10 + half])
        whole = t1[3, half]
        for b in range(3):
            whole = whole + r2[half, b].astype(F32)
        us[half * 4 : half * 4 + 4] = whole.reshape(4, 32, HD).astype(BF16)
    ur[c * NZ + z] = us[z]
    for d in (4, 3, 5, 2, 6, 1, 7):
        other = (z + d) % NZ
        send(us.at[other], ur.at[c * NZ + z], snd.at[19], rcv.at[12], (other * NY + y, h))
        send(us.at[other], ur.at[c * NZ + z], snd.at[19], rcv.at[12], (other * NY + y, x * NC + 1 - c))
    send(us.at[z], ur.at[c * NZ + z], snd.at[19], rcv.at[12], partner)
    settle(hid.at[0], rcv.at[6])
    settle(ur.at[pl.ds(0, 15)], rcv.at[12])
    for t in range(2):
        result = hid[t] + jnp.sum(ur[t * NZ : (t + 1) * NZ].astype(F32), axis=0)
        out[t] = jnp.where(c == 0, result[:, :64], result[:, 64:]).astype(BF16)

    for like, n in (
        (qall.at[pl.ds(0, NS - 1)], 0),
        (ps.at[pl.ds(0, NS - 1)], 1),
        (ss.at[pl.ds(0, NS - 1)], 20),
        (ag.at[pl.ds(0, NS - 1)], 2),
        (hp.at[pl.ds(0, NH - 1)], 3),
        (zb.at[pl.ds(0, NZ - 1)], 4),
        (sqz.at[pl.ds(0, NZ - 1)], 5),
        (hid.at[0], 6),
        (s2.at[0], 7),
        (s2.at[0], 8),
        (ga.at[pl.ds(0, 3)], 9),
        (gb.at[pl.ds(0, 3)], 10),
        (ga, 11),
        (gb, 12),
        (sqx.at[pl.ds(0, NX - 1)], 13),
        (sqy.at[pl.ds(0, NY - 1)], 14),
        (sqp.at[0], 15),
        (sb, 16),
        (s1, 17),
        (s2, 18),
        (ur.at[pl.ds(0, 15)], 19),
    ):
        settle(like, snd.at[n])


def shards(
    lengths,
    block_table,
    slot_request,
    kv_pool,
    new_kv,
    queries,
    residual,
    norm_gain,
    w_out,
    w_gate,
    w_up,
    w_down,
):
    vmem = pl.BlockSpec(memory_space=pltpu.VMEM)
    smem = pl.BlockSpec(memory_space=pltpu.SMEM)
    anywhere = pl.BlockSpec(memory_space=pl.ANY)
    scratch = [
        ((TOKENS, 256), BF16),
        ((TOKENS, HD), BF16),
        ((1024, 512), BF16),
        ((104, 16384), BF16),
        ((104, 16384), BF16),
        ((104, 16384), BF16),
        ((NS, ROWS, HD), BF16),
        ((NS * ROWS, HD), BF16),
        ((PAGE, HD), F32),
        ((NS * ROWS, TOKENS), F32),
        ((NS * ROWS, HD), F32),
        ((NS * ROWS, 256), F32),
        ((NS, ROWS, HD), BF16),
        ((NS, ROWS, HD), BF16),
        ((NS, 1, HD), F32),
        ((NS, 1, HD), F32),
        ((NS, ROWS, HD), BF16),
        ((NS * ROWS, HD), F32),
        ((NH, 32, HD), F32),
        ((NH, 32, HD), F32),
        ((2, 32, HD), F32),
        ((NZ, 32, HD), BF16),
        ((NZ, 1, HD), F32),
        ((NX, 1, HD), F32),
        ((NY, 1, HD), F32),
        ((2, 1, HD), F32),
        ((NY, NX, 128, HD), BF16),
        ((NX, NY, 128, HD), BF16),
        ((NY, NX, 128, HD), BF16),
        ((NX, NY, 128, HD), BF16),
        ((4, 1024, HD), F32),
        ((4, 1024, HD), BF16),
        ((4, 1024, HD), BF16),
        ((4, 6, 128, HD), BF16),
        ((4, 6, 128, HD), BF16),
        ((4, 2, 128, HD), F32),
        ((2, 3, 128, HD), BF16),
        ((2, 3, 128, HD), BF16),
        ((NZ, 32, HD), BF16),
        ((2 * NZ, 32, HD), BF16),
    ]
    return pl.pallas_call(
        kernel,
        out_shape=jax.ShapeDtypeStruct((2, NS, 64), BF16),
        in_specs=[smem, smem] + [vmem] * 5 + [anywhere] * 5,
        out_specs=vmem,
        scratch_shapes=[pltpu.VMEM(shape, kind) for shape, kind in scratch]
        + [
            pltpu.SemaphoreType.DMA(n)
            for n in ((5,), (21,), (14,), (3,), (3,), (4, 3), (4, 3), (16,), (16,), (4,), (4,))
        ],
        compiler_params=pltpu.CompilerParams(
            collective_id=0, has_side_effects=True, vmem_limit_bytes=56 * 1024 * 1024
        ),
    )(
        lengths,
        slot_request,
        block_table,
        new_kv.reshape(3, 256),
        queries.reshape(2, 1024),
        residual,
        norm_gain.reshape(1, 512),
        kv_pool.reshape(TOKENS, 256),
        w_out.reshape(1024, 512),
        w_gate,
        w_up,
        w_down,
    )


def solution(mesh):
    in_specs = (
        P(),
        P(),
        P(),
        P("seq", None, "head", None),
        P(None, "seq", "head", None),
        P(None, "seq", "head", None),
        P(None, None, "seq"),
        P("seq"),
        P("head", None, "seq"),
        P(("seq", "head"), None),
        P(("seq", "head"), None),
        P(("seq", "head"), None),
    )
    out_specs = P(None, None, ("seq", "head"))
    return jax.shard_map(shards, mesh=mesh, in_specs=in_specs, out_specs=out_specs, check_vma=False)
```

time: 93.9 us -> 78 us (0.83)
  Pallas kernels: 92.3 us -> 76.5 us
    pallas_call x1, Pallas kernels: 92.3 us -> 76.5 us  [shards(): pl.pallas_call(kernel, out_shape=jax.ShapeDtypeStruct((2, NS, 64), BF16),...]
where the time goes in v2:
time: 78 us; the launch traced here: 77.8 us
  Pallas kernels  76.5 us (98%)
  local copies, waits for them, and re-layouts  1.32 us (2%)
    pallas_call x1, Pallas kernels, shards(): pl.pallas_call(kernel, out_shape=jax.ShapeDtypeStruct((2, NS, 64), BF16),...  76.5 us

profile of v2, /device:TPU:1, one launch (start us, length us, event | category | flops | bytes accessed | tf_op | source)
XLA Modules:
  0.0 77.8 jit_solution(13325147217293347768)
XLA Ops:
  0.0 76.5 %shard_map.118 = bf16[2,32,64]{2,1,0:T(8,128)(2,1)} custom-call(s32[32]{0:T(128)} %lengths.1, s32[32]{0:T(128)} %slot_request.1, s32[32,256]{1,0:T(8,128)} %table.1, bf16[3,256]{1,0:T(4,128)(2,1)} %bitcast.8, bf16[2,1024]{1,0:T(2,128)(2,1)} %bitcast.7, bf16[2,32,512]{2,1,0:T(8,128)(2,1)} %residual.1, f32[1,512]{1,0:T(1,128)} %bitcast.9, ...), custom_call_target="tpu_custom_call" | custom-call | tf_op jit(solution)/shard_map/pallas_call | solution.py:530
  76.5 1.3 %copy.14 = bf16[2,32,64]{2,1,0:T(8,128)(2,1)} copy(bf16[2,32,64]{2,1,0:T(8,128)(2,1)} %shard_map.118) | data formatting | bytes 16384

commit v3 on v2

v3 whole, which is shorter than its diff:
```python
import functools
import math

import jax
import jax.numpy as jnp
from jax import lax
from jax.experimental import pallas as pl
from jax.experimental.pallas import tpu as pltpu
from jax.sharding import PartitionSpec as P

EPSILON = 1e-05
NZ, NY, NX, NC = 8, 4, 4, 2
NS, NH = NZ * NY, NX * NC
HD = 128
PAGE = 64
ROWS = 16
TOKENS = 4096
CHUNK = 512
APART = (0, 1, 2, 3, 7, 6, 5, 4)
LAG = 12
BATCH, LAST_BATCH = 12, 8
FAR = 131072.0
F32, BF16 = jnp.float32, jnp.bfloat16
NT = (((1,), (1,)), ((), ()))
EXP_SCALE = math.log2(math.e) / math.sqrt(HD)


RING = (1, 3, 2)
AROUND = sorted(
    ((dz, dy) for dz in range(NZ) for dy in range(NY) if dz or dy),
    key=lambda d: -(min(d[0], NZ - d[0]) + min(d[1], NY - d[1])),
)


def iota(shape, dim):
    return lax.broadcasted_iota(jnp.int32, shape, dim)


def kernel(
    lengths, slot_request, new_kv, queries,
    table_hbm, residual_hbm, gain_hbm, kv_hbm, wo_hbm, wg_hbm, wu_hbm, wd_hbm,
    out,
    table, residual, gain, kv, bias, wo, wg, wu, wd,
    qall, hot, codes, scores, peak, acc,
    ps, pr, ss, sr, ag, af, hp, hr, hid,
    sqz, sqx, sqy, sqp, ga, gb, pa, pb,
    o1, sb, rb, s1, r1, t1, fs, fr,
    load_sem, snd, rcv, z_sem, a2, b2, a3, b3, pa_sem, pb_sem, rb_sem, r1_sem,
):
    s = lax.axis_index("seq")
    h = lax.axis_index("head")
    z, y = s // NY, s % NY
    x, c = h // NC, h % NC
    partner = (s, x * NC + 1 - c)

    def shard(dz, dy):
        return ((z + dz) % NZ) * NY + (y + dy) % NY

    def at_y(other):
        return (z * NY + other, h)

    def at_x(other):
        return (s, other * NC + c)

    def send(src, dst, send_sem, recv_sem, device):
        pltpu.make_async_remote_copy(
            src_ref=src,
            dst_ref=dst,
            send_sem=send_sem,
            recv_sem=recv_sem,
            device_id=device,
            device_id_type=pl.DeviceIdType.MESH,
        ).start()

    def settle(like, sem):
        pltpu.make_async_copy(like, like, sem).wait()

    barrier = pltpu.get_barrier_semaphore()

    def greet(device):
        pl.semaphore_signal(barrier, inc=1, device_id=device, device_id_type=pl.DeviceIdType.MESH)

    for dz, dy in AROUND:
        greet((shard(dz, dy), h))

    @pl.loop(1, NH)
    def _(d):
        greet((s, (h + d) % NH))

    @pl.loop(1, NZ)
    def _(d):
        greet((((z + d) % NZ) * NY + y, x * NC + 1 - c))

    loads = [
        pltpu.make_async_copy(src, dst, load_sem.at[n])
        for n, (src, dst) in enumerate(
            (
                (kv_hbm, kv),
                (wo_hbm, wo),
                (wg_hbm, wg),
                (wu_hbm, wu),
                (wd_hbm, wd),
                (table_hbm, table),
                (residual_hbm, residual),
                (gain_hbm, gain),
            )
        )
    ]
    for n in (5, 0, 1, 6, 7, 2, 3, 4):
        loads[n].start()

    wide = queries[...].astype(F32)
    own_query = jnp.concatenate(
        [wide[t : t + 1, g * HD : (g + 1) * HD] for t in range(2) for g in range(8)], axis=0
    )
    qall[s] = own_query.astype(BF16)

    pl.semaphore_wait(barrier, (NS - 1) + (NH - 1) + (NZ - 1))

    for dz, dy in AROUND:
        send(qall.at[s], qall.at[s], snd.at[0], rcv.at[0], (shard(dz, dy), h))

    loads[5].wait()
    row = iota((NS, HD), 0)
    length = jnp.zeros((NS, HD), jnp.int32)
    slot = jnp.zeros((NS, HD), jnp.int32)
    for r in range(NS):
        length = jnp.where(row == r, lengths[r], length)
        slot = jnp.where(row == slot_request[r], r, slot)
    halves = []
    for half in range(2):
        page = iota((NS, HD), 1) + half * HD
        filled = jnp.clip(length - page * PAGE, 0, PAGE)
        local = jnp.where(filled > 0, table[:, half * HD : (half + 1) * HD] - s * PAGE, -1)
        halves.append((local, (slot * HD + filled).astype(F32)))

    def find(p, carry):
        hits = [jnp.where(local == p, code, 0.0) for local, code in halves]
        codes[pl.ds(p, 1), :] = jnp.sum(hits[0] + hits[1], axis=0, keepdims=True)
        return carry

    lax.fori_loop(0, PAGE, find, 0)
    code = jnp.sum(codes[...], axis=1, keepdims=True)
    codes[...] = jnp.broadcast_to(code, (PAGE, HD))

    def cover(p, carry):
        both = codes[pl.ds(p, 1), :].astype(jnp.int32)
        mine = (iota((PAGE, HD), 1) == both // HD) & (iota((PAGE, HD), 0) < both % HD)
        bias[pl.ds(pl.multiple_of(p * PAGE, PAGE), PAGE), :] = jnp.where(mine, 0.0, -FAR).astype(BF16)
        return carry

    lax.fori_loop(0, PAGE, cover, 0)
    hot[...] = jnp.where(iota((NS * ROWS, HD), 0) // ROWS == iota((NS * ROWS, HD), 1), 1.0, 0.0).astype(BF16)

    loads[0].wait()
    settle(qall.at[pl.ds(0, NS - 1)], rcv.at[0])

    aug_query = jnp.concatenate([qall[...].reshape(NS * ROWS, HD), hot[...]], axis=1)
    peak[...] = jnp.full((NS * ROWS, HD), -4.0 * FAR, F32)

    def score(k, carry):
        tokens = pl.ds(pl.multiple_of(k * CHUNK, CHUNK), CHUNK)
        aug_key = jnp.concatenate([kv[tokens, :HD], bias[tokens, :]], axis=1)
        raw = lax.dot_general(aug_query, aug_key, NT, preferred_element_type=F32)
        scores[:, tokens] = raw
        peak[...] = jnp.maximum(peak[...], functools.reduce(jnp.maximum, [raw[:, n : n + HD] for n in range(0, CHUNK, HD)]))
        return carry

    lax.fori_loop(0, TOKENS // CHUNK, score, 0, unroll=True)
    top = jnp.max(peak[...], axis=1, keepdims=True).astype(BF16).astype(F32)
    peak[...] = jnp.broadcast_to(top, (NS * ROWS, HD))
    acc[...] = jnp.zeros((NS * ROWS, 2 * HD), F32)

    def mix(k, carry):
        tokens = pl.ds(pl.multiple_of(k * CHUNK, CHUNK), CHUNK)
        aug_value = jnp.concatenate([kv[tokens, HD:], jnp.ones((CHUNK, HD), BF16)], axis=1)
        base = jnp.concatenate([peak[...]] * (CHUNK // HD), axis=1)
        weights = jnp.exp2((scores[:, tokens] - base) * EXP_SCALE).astype(BF16)
        acc[...] += jnp.dot(weights, aug_value, preferred_element_type=F32)
        return carry

    lax.fori_loop(0, TOKENS // CHUNK, mix, 0, unroll=True)
    acc_rows = acc[:, :HD].astype(BF16).reshape(NS, ROWS, HD)
    ps[...] = acc_rows
    cube = (NS, ROWS, HD)
    lane, line = iota(cube, 2), iota(cube, 1)
    stats = jnp.where(lane == line, peak[...].reshape(cube), 0.0)
    stats = jnp.where(lane == line + ROWS, acc[:, HD:].reshape(cube), stats)
    ss[...] = jnp.sum(stats, axis=1, keepdims=True)
    pr[s] = ps[s]
    sr[s] = ss[s]
    for dz, dy in AROUND:
        other = shard(dz, dy)
        send(ps.at[other], pr.at[s], snd.at[1], rcv.at[1], (other, h))
        send(ss.at[other], sr.at[s], snd.at[20], rcv.at[13], (other, h))

    fresh = new_kv[...].astype(F32)
    late = iota((ROWS, 1), 0) >= ROWS // 2
    rounded_query = own_query.astype(BF16).astype(F32)
    fresh_scores = []
    for e in range(3):
        raw = jnp.sum(rounded_query * fresh[e : e + 1, :HD], axis=1, keepdims=True)
        fresh_scores.append(jnp.where(late, raw, -FAR) if e == 2 else raw)
    settle(pr.at[pl.ds(0, NS - 1)], rcv.at[1])
    settle(sr.at[pl.ds(0, NS - 1)], rcv.at[13])
    stats = jnp.broadcast_to(sr[...], cube)
    tops = jnp.sum(jnp.where(lane == line, stats, 0.0), axis=2, keepdims=True)
    sums = jnp.sum(jnp.where(lane == line + ROWS, stats, 0.0), axis=2, keepdims=True)
    top = jnp.max(tops, axis=0)
    for raw in fresh_scores:
        top = jnp.maximum(top, raw)
    factor = jnp.exp2((tops - top[None]) * EXP_SCALE)
    total = jnp.sum(factor * sums, axis=0)
    mixed = jnp.sum(factor * pr[...].astype(F32), axis=0)
    for e, raw in enumerate(fresh_scores):
        weight = jnp.exp2((raw - top) * EXP_SCALE).astype(BF16).astype(F32)
        total = total + weight
        mixed = mixed + weight * fresh[e : e + 1, HD:]
    ag[s] = (mixed / total).astype(BF16)

    for dz, dy in AROUND:
        send(ag.at[s], ag.at[s], snd.at[2], rcv.at[2], (shard(dz, dy), h))

    loads[1].wait()
    loads[6].wait()
    loads[7].wait()
    settle(ag.at[pl.ds(0, NS - 1)], rcv.at[2])

    af[...] = ag[...].reshape(NS * ROWS, HD).astype(F32)
    attended = jnp.concatenate(
        [
            jnp.concatenate([af[pl.ds(t * 8 + g, NS, stride=ROWS), :] for g in range(8)], axis=1)
            for t in range(2)
        ],
        axis=0,
    ).astype(BF16)
    part = jnp.dot(attended, wo[...], preferred_element_type=F32)
    for xx in range(NX):
        for cc in range(NC):
            hp[xx * NC + cc] = part[cc * NS : (cc + 1) * NS, xx * HD : (xx + 1) * HD]
    hr[h] = hp[h]

    @pl.loop(1, NH)
    def _(d):
        other = (h + d) % NH
        send(hp.at[other], hr.at[h], snd.at[3], rcv.at[3], (s, other))

    columns = pl.ds(pl.multiple_of(x * HD, HD), HD)
    settle(hr.at[pl.ds(0, NH - 1)], rcv.at[3])
    hidden = residual[c, :, columns].astype(F32) + jnp.sum(hr[...], axis=0)
    hid[c] = hidden
    square = jnp.sum(hidden * hidden, axis=1, keepdims=True)
    halves = ((ga, pa, a2, a3, pa_sem, x, y, at_x, at_y), (gb, pb, b2, b3, pb_sem, y, x, at_y, at_x))
    ga[y, x, 0:32] = (hidden * gain[:, columns]).astype(BF16)
    spread = jnp.where(iota((NS, HD), 0) == iota((NS, HD), 1), square, 0.0)
    sqz[z] = jnp.sum(spread, axis=0, keepdims=True)
    own = ga.at[y, x, pl.ds(0, 32)]
    for p in range(1, NZ):
        there = (((z + NZ - APART[p]) % NZ) * NY + y, h)
        place = ga.at[y, x, pl.ds(p * 32, 32)] if p < 4 else gb.at[x, y, pl.ds((p - 4) * 32, 32)]
        send(own, place, snd.at[4], z_sem.at[p // 2], there)
    for d in (4, 3, 5, 2, 6, 1, 7):
        there = (((z + d) % NZ) * NY + y, h)
        send(sqz.at[z], sqz.at[z], snd.at[5], rcv.at[5], there)
    send(hid.at[c], hid.at[c], snd.at[6], rcv.at[6], partner)
    done = []

    def block(ref, outer, inner, w):
        return ref.at[outer, inner, pl.ds(w * 64, 64)]

    def pass_on(half, w, inner, n):
        full, _, _, last, _, _, outer, _, at_last = halves[half]
        here = block(full, outer, inner, w)
        for d in RING:
            send(here, here, snd.at[9 + half], last.at[w, n, d - 1], at_last((outer + d) % 4))
        cross(half, w, outer, inner, n)

    def cross(half, w, outer, inner, n):
        full, other, _, _, sem, _, _, _, _ = halves[half]
        send(block(full, outer, inner, w), block(other, outer, inner, w), snd.at[11 + half], sem.at[w, n], partner)
        done.append((half, w, outer, inner, n))

    for w in range(2):
        for half in range(2):
            full, _, first, _, _, inner, outer, at_first, _ = halves[half]
            here = block(full, outer, inner, w)
            if half == 0 and w == 0:
                settle(own, z_sem.at[0])
            else:
                settle(here, z_sem.at[half * 2 + w])
            for d in RING:
                send(here, here, snd.at[7 + half], first.at[w, d - 1], at_first((inner + d) % 4))
            pass_on(half, w, inner, 0)
    settle(sqz.at[pl.ds(0, NZ - 1)], rcv.at[5])
    sqx[x] = jnp.sum(sqz[...], axis=0)
    for d in RING:
        send(sqx.at[x], sqx.at[x], snd.at[13], rcv.at[7], at_x((x + d) % NX))

    loads[2].wait()
    loads[3].wait()

    def multiply(items, sums):
        for half, w, outer, inner, n in items:
            full, other, _, _, sem, _, _, _, _ = halves[half]
            settle(block(other, outer, inner, w), sem.at[w, n])
        gate, up = sums
        for half, w, outer, inner, n in items:
            full, other, _, _, _, _, _, _, _ = halves[half]
            yy, xx = (inner, outer) if half else (outer, inner)
            both = (2 * w, 2 * w + 1)
            stream = jnp.concatenate(
                [
                    jnp.concatenate([ref[outer, inner, p * 32 : (p + 1) * 32] for p in both], axis=1)
                    for ref in (full, other)
                ],
                axis=0,
            )
            zs = [(z + APART[half * 4 + p]) % NZ for p in both]
            where = [pl.ds(pl.multiple_of(zz * 2048 + yy * 512 + xx * HD, HD), HD) for zz in zs]
            left = [jnp.concatenate([ref[:, at] for at in where], axis=1) for ref in (wg, wu)]
            gate = gate + lax.dot_general(left[0], stream, NT, preferred_element_type=F32)
            up = up + lax.dot_general(left[1], stream, NT, preferred_element_type=F32)
        return gate, up

    def catch_up(lag, batch, sums):
        while len(done) >= lag + batch:
            sums = multiply([done.pop(0) for _ in range(batch)], sums)
        return sums

    sums = (jnp.zeros((104, 64), F32), jnp.zeros((104, 64), F32))

    def last_arrivals(w, half, n, k):
        full, _, _, last, _, inner, outer, _, _ = halves[half]
        for d in RING:
            there, beside = (outer + 4 - d) % 4, (inner + 4 - k) % 4
            settle(block(full, there, beside, w), last.at[w, n, d - 1])
            cross(half, w, there, beside, 3 * n + 3 + d)

    for w in range(2):
        for half in range(2):
            full, _, first, _, _, inner, outer, _, _ = halves[half]
            for n, d in enumerate(RING):
                beside = (inner + 4 - d) % 4
                settle(block(full, outer, beside, w), first.at[w, d - 1])
                pass_on(half, w, beside, n + 1)
        for half in range(2):
            last_arrivals(w, half, 0, 0)
    settle(sqx.at[pl.ds(0, NX - 1)], rcv.at[7])
    sqy[y] = jnp.sum(sqx[...], axis=0)
    for d in RING:
        send(sqy.at[y], sqy.at[y], snd.at[14], rcv.at[8], at_y((y + d) % NY))
    sums = catch_up(LAG, BATCH, sums)
    for w in range(2):
        for n, k in enumerate(RING):
            for half in range(2):
                last_arrivals(w, half, n + 1, k)
                sums = catch_up(LAG, BATCH, sums)
        if w == 0:
            settle(sqy.at[pl.ds(0, NY - 1)], rcv.at[8])
            sqp[0] = jnp.sum(sqy[...], axis=0)
            send(sqp.at[0], sqp.at[1], snd.at[15], rcv.at[9], partner)
    sums = catch_up(LAST_BATCH, BATCH, sums)
    while done:
        sums = catch_up(0, min(LAST_BATCH, len(done)), sums)
    settle(sqp.at[0], rcv.at[9])
    square = jnp.broadcast_to(sqp[0], (8, HD)) + pltpu.roll(jnp.broadcast_to(sqp[1], (8, HD)), 32, 1)
    scale = lax.rsqrt(square[0:1, 0:64] * (1.0 / 16384.0) + EPSILON)
    gate = sums[0] * scale
    up = sums[1] * scale
    activation = (gate / (1.0 + jnp.exp(-gate)) * up).T.astype(BF16)

    loads[4].wait()
    turn = (2, 1, 3, 0)
    spots = [[(y + b) % NY, (x + b) % NX] for b in turn]

    def groups(r):
        k, first = r % 4, r // 4 * 4
        return [(spots[b][0], spots[k][1], first) for b in range(4)] + [
            (spots[k][0], spots[b][1], first + 2) for b in range(4)
        ]

    def down(r):
        for m, (yy, xx, first) in enumerate(groups(r)):
            weight = jnp.concatenate(
                [
                    wd[:, pl.ds(pl.multiple_of((first + zz) * 2048 + yy * 512 + xx * HD, HD), HD)]
                    for zz in range(2)
                ],
                axis=1,
            )
            product = jnp.dot(activation, weight, preferred_element_type=F32)
            for zz in range(2):
                at = slice(m * 64 + zz * 32, m * 64 + (zz + 1) * 32)
                piece = product[:, zz * HD : (zz + 1) * HD]
                o1[r, at] = piece[0:32]
                sb[r, at] = piece[32:64].astype(BF16)
        send(sb.at[r], rb.at[r], snd.at[16], rb_sem.at[r], partner)

    def finish(r):
        settle(rb.at[r], rb_sem.at[r])
        for half in range(2):
            for b in range(4):
                at = slice((half * 4 + b) * 64, (half * 4 + b + 1) * 64)
                whole = o1[r, at] + rb[r, at].astype(F32)
                if b == 3:
                    t1[r, half] = whole
                else:
                    s1[r, half * 3 + b] = whole.astype(BF16)
                    there = at_x(spots[b][1]) if half else at_y(spots[b][0])
                    send(s1.at[r, half * 3 + b], r1.at[r, half * 3 + b], snd.at[17], r1_sem.at[r], there)

    def reduce_one(r):
        k = r % 4
        settle(r1.at[r], r1_sem.at[r])
        low = iota((16, HD), 1) < 64
        for half in range(2):
            whole = t1[r, half]
            for b in range(3):
                whole = whole + r1[r, half * 3 + b].astype(F32)
            for zz in range(2):
                top, bottom = whole[zz * 32 : zz * 32 + 16], whole[zz * 32 + 16 : zz * 32 + 32]
                fs[r, half, zz, 0] = jnp.where(low, top, pltpu.roll(bottom, 64, 1)).astype(BF16)
                fs[r, half, zz, 1] = jnp.where(low, pltpu.roll(top, 64, 1), bottom).astype(BF16)
            yy, xx = (spots[k][0], x) if half else (y, spots[k][1])
            for zz in range(2):
                owner_z = r // 4 * 4 + half * 2 + zz
                for cc in range(2):

                    def go(zz=zz, cc=cc, owner_z=owner_z):
                        send(
                            fs.at[r, half, zz, cc],
                            fr.at[(c * NZ + z) * 4 + k],
                            snd.at[18],
                            rcv.at[10],
                            (owner_z * NY + yy, xx * NC + cc),
                        )

                    if k == 3:
                        pl.when((owner_z != z) | (cc != c))(go)
                    else:
                        go()

    for r in range(8):
        down(r)
        if r >= 2:
            finish(r - 2)
    for r in range(6, 8):
        finish(r)
    for r in range(4):
        reduce_one(r)
    for r in range(4, 8):
        reduce_one(r)
    fr[(c * NZ + z) * 4 + 3] = fs[z // 4 * 4 + 3, z % 4 // 2, z % 2, c]
    settle(hid.at[0], rcv.at[6])
    settle(fr.at[pl.ds(0, 63)], rcv.at[10])
    for t in range(2):
        added = jnp.sum(fr[t * 32 : (t + 1) * 32].astype(F32), axis=0)
        base = jnp.where(c == 0, hid[t, :, :64], hid[t, :, 64:])
        out[t, 0:16] = (base[0:16] + added[:, :64]).astype(BF16)
        out[t, 16:32] = (base[16:32] + added[:, 64:]).astype(BF16)

    for like, n in (
        (qall.at[pl.ds(0, NS - 1)], 0),
        (ps.at[pl.ds(0, NS - 1)], 1),
        (ss.at[pl.ds(0, NS - 1)], 20),
        (ag.at[pl.ds(0, NS - 1)], 2),
        (hp.at[pl.ds(0, NH - 1)], 3),
        (kv.at[pl.ds(0, 112)], 4),
        (sqz.at[pl.ds(0, NZ - 1)], 5),
        (hid.at[0], 6),
        (ga.at[0, pl.ds(0, 3)], 7),
        (gb.at[0, pl.ds(0, 3)], 8),
        (ga.at[pl.ds(0, 3)], 9),
        (gb.at[pl.ds(0, 3)], 10),
        (ga, 11),
        (gb, 12),
        (sqx.at[pl.ds(0, NX - 1)], 13),
        (sqy.at[pl.ds(0, NY - 1)], 14),
        (sqp.at[0], 15),
        (sb, 16),
        (s1, 17),
        (fr.at[pl.ds(0, 63)], 18),
    ):
        settle(like, snd.at[n])


def shards(
    lengths,
    block_table,
    slot_request,
    kv_pool,
    new_kv,
    queries,
    residual,
    norm_gain,
    w_out,
    w_gate,
    w_up,
    w_down,
):
    vmem = pl.BlockSpec(memory_space=pltpu.VMEM)
    smem = pl.BlockSpec(memory_space=pltpu.SMEM)
    anywhere = pl.BlockSpec(memory_space=pl.ANY)
    scratch = [
        ((NS, 256), jnp.int32),
        ((2, NS, 512), BF16),
        ((1, 512), F32),
        ((TOKENS, 256), BF16),
        ((TOKENS, HD), BF16),
        ((1024, 512), BF16),
        ((104, 16384), BF16),
        ((104, 16384), BF16),
        ((104, 16384), BF16),
        ((NS, ROWS, HD), BF16),
        ((NS * ROWS, HD), BF16),
        ((PAGE, HD), F32),
        ((NS * ROWS, TOKENS), F32),
        ((NS * ROWS, HD), F32),
        ((NS * ROWS, 256), F32),
        ((NS, ROWS, HD), BF16),
        ((NS, ROWS, HD), BF16),
        ((NS, 1, HD), F32),
        ((NS, 1, HD), F32),
        ((NS, ROWS, HD), BF16),
        ((NS * ROWS, HD), F32),
        ((NH, 32, HD), F32),
        ((NH, 32, HD), F32),
        ((2, 32, HD), F32),
        ((NZ, 1, HD), F32),
        ((NX, 1, HD), F32),
        ((NY, 1, HD), F32),
        ((2, 1, HD), F32),
        ((NY, NX, 128, HD), BF16),
        ((NX, NY, 128, HD), BF16),
        ((NY, NX, 128, HD), BF16),
        ((NX, NY, 128, HD), BF16),
        ((8, 512, HD), F32),
        ((8, 512, HD), BF16),
        ((8, 512, HD), BF16),
        ((8, 6, 64, HD), BF16),
        ((8, 6, 64, HD), BF16),
        ((8, 2, 64, HD), F32),
        ((8, 2, 2, 2, 16, HD), BF16),
        ((64, 16, HD), BF16),
    ]
    return pl.pallas_call(
        kernel,
        out_shape=jax.ShapeDtypeStruct((2, NS, 64), BF16),
        in_specs=[smem, smem, vmem, vmem] + [anywhere] * 8,
        out_specs=vmem,
        scratch_shapes=[pltpu.VMEM(shape, kind) for shape, kind in scratch]
        + [
            pltpu.SemaphoreType.DMA(n)
            for n in ((8,), (21,), (14,), (4,), (2, 3), (2, 3), (2, 4, 3), (2, 4, 3), (2, 16), (2, 16), (8,), (8,))
        ],
        compiler_params=pltpu.CompilerParams(
            collective_id=0, has_side_effects=True, vmem_limit_bytes=56 * 1024 * 1024
        ),
    )(
        lengths,
        slot_request,
        new_kv.reshape(3, 256),
        queries.reshape(2, 1024),
        block_table,
        residual,
        norm_gain.reshape(1, 512),
        kv_pool.reshape(TOKENS, 256),
        w_out.reshape(1024, 512),
        w_gate,
        w_up,
        w_down,
    )


def solution(mesh):
    in_specs = (
        P(),
        P(),
        P(),
        P("seq", None, "head", None),
        P(None, "seq", "head", None),
        P(None, "seq", "head", None),
        P(None, None, "seq"),
        P("seq"),
        P("head", None, "seq"),
        P(("seq", "head"), None),
        P(("seq", "head"), None),
        P(("seq", "head"), None),
    )
    out_specs = P(None, None, ("seq", "head"))
    return jax.shard_map(shards, mesh=mesh, in_specs=in_specs, out_specs=out_specs, check_vma=False)
```

time: 78 us -> 74 us (0.949)
  Pallas kernels: 76.5 us -> 72.4 us
    pallas_call x1, Pallas kernels: 76.5 us -> 72.4 us  [shards(): pl.pallas_call(kernel, out_shape=jax.ShapeDtypeStruct((2, NS, 64), BF16),...]
where the time goes in v3:
time: 74 us; the launch traced here: 73.7 us
  Pallas kernels  72.4 us (98%)
  local copies, waits for them, and re-layouts  1.32 us (2%)
    pallas_call x1, Pallas kernels, shards(): pl.pallas_call(kernel, out_shape=jax.ShapeDtypeStruct((2, NS, 64), BF16),...  72.4 us

profile of v3, /device:TPU:1, one launch (start us, length us, event | category | flops | bytes accessed | tf_op | source)
XLA Modules:
  0.0 73.7 jit_solution(7854770861709107961)
XLA Ops:
  0.0 72.4 %shard_map.118 = bf16[2,32,64]{2,1,0:T(8,128)(2,1)} custom-call(s32[32]{0:T(128)} %lengths.1, s32[32]{0:T(128)} %slot_request.1, bf16[3,256]{1,0:T(4,128)(2,1)} %bitcast.8, bf16[2,1024]{1,0:T(2,128)(2,1)} %bitcast.7, s32[32,256]{1,0:T(8,128)} %table_hbm.1, bf16[2,32,512]{2,1,0:T(8,128)(2,1)} %residual_hbm.1, f32[1,512]{1,0:T(1,128)} %bitcast.9, ...), custom_call_target="tpu_custom_call" | custom-call | tf_op jit(solution)/shard_map/pallas_call | solution.py:546
  72.4 1.3 %copy.14 = bf16[2,32,64]{2,1,0:T(8,128)(2,1)} copy(bf16[2,32,64]{2,1,0:T(8,128)(2,1)} %shard_map.118) | data formatting | bytes 16384

commit v4 on v3

--- a/solution.py
+++ b/solution.py
@@ -26,10 +26,13 @@
 
 
 RING = (1, 3, 2)
-AROUND = sorted(
-    ((dz, dy) for dz in range(NZ) for dy in range(NY) if dz or dy),
-    key=lambda d: -(min(d[0], NZ - d[0]) + min(d[1], NY - d[1])),
+NEAR = sorted(
+    ((dz, dy) for dz in range(NZ) for dy in range(NY)),
+    key=lambda d: min(d[0], NZ - d[0]) + min(d[1], NY - d[1]),
 )
+SEEN = [NEAR.index(((NZ - dz) % NZ, (NY - dy) % NY)) for dz, dy in NEAR]
+AROUND = NEAR[:0:-1]
+HALF = NS // 2
 
 
 def iota(shape, dim):
@@ -37,10 +40,9 @@
 
 
 def kernel(
-    lengths, slot_request, new_kv, queries,
-    table_hbm, residual_hbm, gain_hbm, kv_hbm, wo_hbm, wg_hbm, wu_hbm, wd_hbm,
+    lengths_hbm, slot_hbm, new_hbm, queries_hbm, table_hbm, residual_hbm, gain_hbm, kv_hbm, wo_hbm, wg_hbm, wu_hbm, wd_hbm,
     out,
-    table, residual, gain, kv, bias, wo, wg, wu, wd,
+    lengths, slot_request, new_kv, queries, table, residual, gain, kv, bias, wo, wg, wu, wd,
     qall, hot, codes, scores, peak, acc,
     ps, pr, ss, sr, ag, af, hp, hr, hid,
     sqz, sqx, sqy, sqp, ga, gb, pa, pb,
@@ -103,30 +105,37 @@
                 (table_hbm, table),
                 (residual_hbm, residual),
                 (gain_hbm, gain),
+                (lengths_hbm, lengths),
+                (slot_hbm, slot_request),
+                (new_hbm, new_kv),
+                (queries_hbm, queries),
             )
         )
     ]
-    for n in (5, 0, 1, 6, 7, 2, 3, 4):
+    for n in (11, 8, 9, 5, 0, 10, 1, 6, 7, 2, 3, 4):
         loads[n].start()
 
+    loads[11].wait()
     wide = queries[...].astype(F32)
     own_query = jnp.concatenate(
         [wide[t : t + 1, g * HD : (g + 1) * HD] for t in range(2) for g in range(8)], axis=0
     )
-    qall[s] = own_query.astype(BF16)
+    qall[0] = own_query.astype(BF16)
 
     pl.semaphore_wait(barrier, (NS - 1) + (NH - 1) + (NZ - 1))
 
-    for dz, dy in AROUND:
-        send(qall.at[s], qall.at[s], snd.at[0], rcv.at[0], (shard(dz, dy), h))
-
-    loads[5].wait()
+    for n in range(1, NS):
+        m = SEEN[n]
+        send(qall.at[0], qall.at[m], snd.at[0], rcv.at[0 if m < HALF else 14], (shard(*NEAR[n]), h))
+
+    for n in (8, 9, 5):
+        loads[n].wait()
     row = iota((NS, HD), 0)
     length = jnp.zeros((NS, HD), jnp.int32)
     slot = jnp.zeros((NS, HD), jnp.int32)
     for r in range(NS):
         length = jnp.where(row == r, lengths[r], length)
-        slot = jnp.where(row == slot_request[r], r, slot)
+        slot = jnp.where(row == slot_request[shard(*NEAR[r])], r, slot)
     halves = []
     for half in range(2):
         page = iota((NS, HD), 1) + half * HD
@@ -139,7 +148,7 @@
         codes[pl.ds(p, 1), :] = jnp.sum(hits[0] + hits[1], axis=0, keepdims=True)
         return carry
 
-    lax.fori_loop(0, PAGE, find, 0)
+    lax.fori_loop(0, PAGE, find, 0, unroll=4)
     code = jnp.sum(codes[...], axis=1, keepdims=True)
     codes[...] = jnp.broadcast_to(code, (PAGE, HD))
 
@@ -149,51 +158,54 @@
         bias[pl.ds(pl.multiple_of(p * PAGE, PAGE), PAGE), :] = jnp.where(mine, 0.0, -FAR).astype(BF16)
         return carry
 
-    lax.fori_loop(0, PAGE, cover, 0)
+    lax.fori_loop(0, PAGE, cover, 0, unroll=4)
     hot[...] = jnp.where(iota((NS * ROWS, HD), 0) // ROWS == iota((NS * ROWS, HD), 1), 1.0, 0.0).astype(BF16)
 
+    def attend(half):
+        slots = slice(half * HALF, (half + 1) * HALF)
+        rows = slice(half * HALF * ROWS, (half + 1) * HALF * ROWS)
+        count = HALF * ROWS
+        aug_query = jnp.concatenate([qall[slots].reshape(count, HD), hot[rows]], axis=1)
+        peak[rows] = jnp.full((count, HD), -4.0 * FAR, F32)
+        for k in range(TOKENS // CHUNK):
+            tokens = slice(k * CHUNK, (k + 1) * CHUNK)
+            aug_key = jnp.concatenate([kv[tokens, :HD], bias[tokens]], axis=1)
+            raw = lax.dot_general(aug_query, aug_key, NT, preferred_element_type=F32)
+            scores[rows, tokens] = raw
+            best = functools.reduce(jnp.maximum, [raw[:, n : n + HD] for n in range(0, CHUNK, HD)])
+            peak[rows] = jnp.maximum(peak[rows], best)
+        top = jnp.max(peak[rows], axis=1, keepdims=True)
+        peak[rows] = jnp.broadcast_to(top, (count, HD))
+        acc[rows] = jnp.zeros((count, 2 * HD), F32)
+        for k in range(TOKENS // CHUNK):
+            tokens = slice(k * CHUNK, (k + 1) * CHUNK)
+            aug_value = jnp.concatenate([kv[tokens, HD:], jnp.ones((CHUNK, HD), BF16)], axis=1)
+            base = jnp.concatenate([peak[rows]] * (CHUNK // HD), axis=1)
+            weights = jnp.exp2((scores[rows, tokens] - base) * EXP_SCALE).astype(BF16)
+            acc[rows] += jnp.dot(weights, aug_value, preferred_element_type=F32)
+        cube = (HALF, ROWS, HD)
+        ps[slots] = acc[rows, :HD].astype(BF16).reshape(cube)
+        lane, line = iota(cube, 2), iota(cube, 1)
+        stats = jnp.where(lane == line, peak[rows].reshape(cube), 0.0)
+        stats = jnp.where(lane == line + ROWS, acc[rows, HD:].reshape(cube), stats)
+        ss[slots] = jnp.sum(stats, axis=1, keepdims=True)
+        if half == 0:
+            pr[0] = ps[0]
+            sr[0] = ss[0]
+        for n in range((half + 1) * HALF - 1, max(half * HALF, 1) - 1, -1):
+            there = (shard(*NEAR[n]), h)
+            send(ps.at[n], pr.at[SEEN[n]], snd.at[1], rcv.at[1], there)
+            send(ss.at[n], sr.at[SEEN[n]], snd.at[20], rcv.at[13], there)
+
     loads[0].wait()
-    settle(qall.at[pl.ds(0, NS - 1)], rcv.at[0])
-
-    aug_query = jnp.concatenate([qall[...].reshape(NS * ROWS, HD), hot[...]], axis=1)
-    peak[...] = jnp.full((NS * ROWS, HD), -4.0 * FAR, F32)
-
-    def score(k, carry):
-        tokens = pl.ds(pl.multiple_of(k * CHUNK, CHUNK), CHUNK)
-        aug_key = jnp.concatenate([kv[tokens, :HD], bias[tokens, :]], axis=1)
-        raw = lax.dot_general(aug_query, aug_key, NT, preferred_element_type=F32)
-        scores[:, tokens] = raw
-        peak[...] = jnp.maximum(peak[...], functools.reduce(jnp.maximum, [raw[:, n : n + HD] for n in range(0, CHUNK, HD)]))
-        return carry
-
-    lax.fori_loop(0, TOKENS // CHUNK, score, 0, unroll=True)
-    top = jnp.max(peak[...], axis=1, keepdims=True).astype(BF16).astype(F32)
-    peak[...] = jnp.broadcast_to(top, (NS * ROWS, HD))
-    acc[...] = jnp.zeros((NS * ROWS, 2 * HD), F32)
-
-    def mix(k, carry):
-        tokens = pl.ds(pl.multiple_of(k * CHUNK, CHUNK), CHUNK)
-        aug_value = jnp.concatenate([kv[tokens, HD:], jnp.ones((CHUNK, HD), BF16)], axis=1)
-        base = jnp.concatenate([peak[...]] * (CHUNK // HD), axis=1)
-        weights = jnp.exp2((scores[:, tokens] - base) * EXP_SCALE).astype(BF16)
-        acc[...] += jnp.dot(weights, aug_value, preferred_element_type=F32)
-        return carry
-
-    lax.fori_loop(0, TOKENS // CHUNK, mix, 0, unroll=True)
-    acc_rows = acc[:, :HD].astype(BF16).reshape(NS, ROWS, HD)
-    ps[...] = acc_rows
+    settle(qall.at[pl.ds(1, HALF - 1)], rcv.at[0])
+    attend(0)
+    settle(qall.at[pl.ds(HALF, HALF)], rcv.at[14])
+    attend(1)
     cube = (NS, ROWS, HD)
     lane, line = iota(cube, 2), iota(cube, 1)
-    stats = jnp.where(lane == line, peak[...].reshape(cube), 0.0)
-    stats = jnp.where(lane == line + ROWS, acc[:, HD:].reshape(cube), stats)
-    ss[...] = jnp.sum(stats, axis=1, keepdims=True)
-    pr[s] = ps[s]
-    sr[s] = ss[s]
-    for dz, dy in AROUND:
-        other = shard(dz, dy)
-        send(ps.at[other], pr.at[s], snd.at[1], rcv.at[1], (other, h))
-        send(ss.at[other], sr.at[s], snd.at[20], rcv.at[13], (other, h))
-
+
+    loads[10].wait()
     fresh = new_kv[...].astype(F32)
     late = iota((ROWS, 1), 0) >= ROWS // 2
     rounded_query = own_query.astype(BF16).astype(F32)
@@ -237,7 +249,8 @@
     part = jnp.dot(attended, wo[...], preferred_element_type=F32)
     for xx in range(NX):
         for cc in range(NC):
-            hp[xx * NC + cc] = part[cc * NS : (cc + 1) * NS, xx * HD : (xx + 1) * HD]
+            piece = part[cc * NS : (cc + 1) * NS, xx * HD : (xx + 1) * HD]
+            hp[xx * NC + cc] = piece.astype(BF16)
     hr[h] = hp[h]
 
     @pl.loop(1, NH)
@@ -247,7 +260,7 @@
 
     columns = pl.ds(pl.multiple_of(x * HD, HD), HD)
     settle(hr.at[pl.ds(0, NH - 1)], rcv.at[3])
-    hidden = residual[c, :, columns].astype(F32) + jnp.sum(hr[...], axis=0)
+    hidden = residual[c, :, columns].astype(F32) + jnp.sum(hr[...].astype(F32), axis=0)
     hid[c] = hidden
     square = jnp.sum(hidden * hidden, axis=1, keepdims=True)
     halves = ((ga, pa, a2, a3, pa_sem, x, y, at_x, at_y), (gb, pb, b2, b3, pb_sem, y, x, at_y, at_x))
@@ -456,8 +469,8 @@
     for t in range(2):
         added = jnp.sum(fr[t * 32 : (t + 1) * 32].astype(F32), axis=0)
         base = jnp.where(c == 0, hid[t, :, :64], hid[t, :, 64:])
-        out[t, 0:16] = (base[0:16] + added[:, :64]).astype(BF16)
-        out[t, 16:32] = (base[16:32] + added[:, 64:]).astype(BF16)
+        out[t, 0:16] = base[0:16] + added[:, :64]
+        out[t, 16:32] = base[16:32] + added[:, 64:]
 
     for like, n in (
         (qall.at[pl.ds(0, NS - 1)], 0),
@@ -499,9 +512,10 @@
     w_down,
 ):
     vmem = pl.BlockSpec(memory_space=pltpu.VMEM)
-    smem = pl.BlockSpec(memory_space=pltpu.SMEM)
     anywhere = pl.BlockSpec(memory_space=pl.ANY)
     scratch = [
+        ((3, 256), BF16),
+        ((2, 1024), BF16),
         ((NS, 256), jnp.int32),
         ((2, NS, 512), BF16),
         ((1, 512), F32),
@@ -523,8 +537,8 @@
         ((NS, 1, HD), F32),
         ((NS, ROWS, HD), BF16),
         ((NS * ROWS, HD), F32),
-        ((NH, 32, HD), F32),
-        ((NH, 32, HD), F32),
+        ((NH, 32, HD), BF16),
+        ((NH, 32, HD), BF16),
         ((2, 32, HD), F32),
         ((NZ, 1, HD), F32),
         ((NX, 1, HD), F32),
@@ -545,13 +559,14 @@
     ]
     return pl.pallas_call(
         kernel,
-        out_shape=jax.ShapeDtypeStruct((2, NS, 64), BF16),
-        in_specs=[smem, smem, vmem, vmem] + [anywhere] * 8,
+        out_shape=jax.ShapeDtypeStruct((2, NS, 64), F32),
+        in_specs=[anywhere] * 12,
         out_specs=vmem,
-        scratch_shapes=[pltpu.VMEM(shape, kind) for shape, kind in scratch]
+        scratch_shapes=[pltpu.SMEM((NS,), jnp.int32)] * 2
+        + [pltpu.VMEM(shape, kind) for shape, kind in scratch]
         + [
             pltpu.SemaphoreType.DMA(n)
-            for n in ((8,), (21,), (14,), (4,), (2, 3), (2, 3), (2, 4, 3), (2, 4, 3), (2, 16), (2, 16), (8,), (8,))
+            for n in ((12,), (21,), (15,), (4,), (2, 3), (2, 3), (2, 4, 3), (2, 4, 3), (2, 16), (2, 16), (8,), (8,))
         ],
         compiler_params=pltpu.CompilerParams(
             collective_id=0, has_side_effects=True, vmem_limit_bytes=56 * 1024 * 1024
@@ -569,7 +584,7 @@
         w_gate,
         w_up,
         w_down,
-    )
+    ).astype(BF16)
 
 
 def solution(mesh):

time: 74 us -> 71 us (0.959)
  Pallas kernels: 72.4 us -> 69.4 us
  other arithmetic: 0 us -> 1.37 us
  local copies, waits for them, and re-layouts: 1.32 us -> 0 us
    pallas_call x1, Pallas kernels: 72.4 us -> 69.4 us  [shards(): pl.pallas_call(kernel, out_shape=jax.ShapeDtypeStruct((2, NS, 64), F32),...]
    convert_element_type x0 -> x1, other arithmetic: none -> 1.37 us  [shards(): return pl.pallas_call(kernel, out_shape=jax.ShapeDtypeStruct((2, NS, 64),...]
    unnamed x1 -> x0, local copies, waits for them, and re-layouts: 1.32 us -> none
where the time goes in v4:
time: 71 us; the launch traced here: 70.8 us
  Pallas kernels  69.4 us (98%)
  other arithmetic  1.37 us (2%)
    pallas_call x1, Pallas kernels, shards(): pl.pallas_call(kernel, out_shape=jax.ShapeDtypeStruct((2, NS, 64), F32),...  69.4 us

profile of v4, /device:TPU:1, one launch (start us, length us, event | category | flops | bytes accessed | tf_op | source)
XLA Modules:
  0.0 70.8 jit_solution(8380718653203058434)
XLA Ops:
  0.0 69.4 %shard_map.118 = f32[2,32,64]{2,1,0:T(8,128)} custom-call(s32[32]{0:T(128)} %lengths_hbm.1, s32[32]{0:T(128)} %slot_hbm.1, bf16[3,256]{1,0:T(4,128)(2,1)} %bitcast.8, bf16[2,1024]{1,0:T(2,128)(2,1)} %bitcast.7, s32[32,256]{1,0:T(8,128)} %table_hbm.1, bf16[2,32,512]{2,1,0:T(8,128)(2,1)} %residual_hbm.1, f32[1,512]{1,0:T(1,128)} %bitcast.9, ...), custom_call_target="tpu_custom_call" | custom-call | tf_op jit(solution)/shard_map/pallas_call | solution.py:560
  69.4 1.4 %convert_element_type.3 = bf16[2,32,64]{2,1,0:T(8,128)(2,1)} convert(f32[2,32,64]{2,1,0:T(8,128)} %shard_map.118) | non-fusion elementwise | flops 4096 | bytes 24576 | tf_op jit(solution)/shard_map/convert_element_type | solution.py:587

commit v5 on v4

--- a/solution.py
+++ b/solution.py
@@ -16,15 +16,17 @@
 ROWS = 16
 TOKENS = 4096
 CHUNK = 512
+WIDE = 2048
 APART = (0, 1, 2, 3, 7, 6, 5, 4)
-LAG = 12
-BATCH, LAST_BATCH = 12, 8
+LAG = 16
+BATCH, LAST_BATCH = 4, 4
 FAR = 131072.0
 F32, BF16 = jnp.float32, jnp.bfloat16
 NT = (((1,), (1,)), ((), ()))
 EXP_SCALE = math.log2(math.e) / math.sqrt(HD)
 
 
+OUT = (2, 1, 3)
 RING = (1, 3, 2)
 NEAR = sorted(
     ((dz, dy) for dz in range(NZ) for dy in range(NY)),
@@ -176,13 +178,14 @@
             peak[rows] = jnp.maximum(peak[rows], best)
         top = jnp.max(peak[rows], axis=1, keepdims=True)
         peak[rows] = jnp.broadcast_to(top, (count, HD))
-        acc[rows] = jnp.zeros((count, 2 * HD), F32)
-        for k in range(TOKENS // CHUNK):
-            tokens = slice(k * CHUNK, (k + 1) * CHUNK)
-            aug_value = jnp.concatenate([kv[tokens, HD:], jnp.ones((CHUNK, HD), BF16)], axis=1)
-            base = jnp.concatenate([peak[rows]] * (CHUNK // HD), axis=1)
+        total = jnp.zeros((count, 2 * HD), F32)
+        for k in range(TOKENS // WIDE):
+            tokens = slice(k * WIDE, (k + 1) * WIDE)
+            aug_value = jnp.concatenate([kv[tokens, HD:], jnp.ones((WIDE, HD), BF16)], axis=1)
+            base = jnp.concatenate([peak[rows]] * (WIDE // HD), axis=1)
             weights = jnp.exp2((scores[rows, tokens] - base) * EXP_SCALE).astype(BF16)
-            acc[rows] += jnp.dot(weights, aug_value, preferred_element_type=F32)
+            total = total + jnp.dot(weights, aug_value, preferred_element_type=F32)
+        acc[rows] = total
         cube = (HALF, ROWS, HD)
         ps[slots] = acc[rows, :HD].astype(BF16).reshape(cube)
         lane, line = iota(cube, 2), iota(cube, 1)
@@ -284,7 +287,7 @@
     def pass_on(half, w, inner, n):
         full, _, _, last, _, _, outer, _, at_last = halves[half]
         here = block(full, outer, inner, w)
-        for d in RING:
+        for d in OUT:
             send(here, here, snd.at[9 + half], last.at[w, n, d - 1], at_last((outer + d) % 4))
         cross(half, w, outer, inner, n)
 
@@ -301,7 +304,7 @@
                 settle(own, z_sem.at[0])
             else:
                 settle(here, z_sem.at[half * 2 + w])
-            for d in RING:
+            for d in OUT:
                 send(here, here, snd.at[7 + half], first.at[w, d - 1], at_first((inner + d) % 4))
             pass_on(half, w, inner, 0)
     settle(sqz.at[pl.ds(0, NZ - 1)], rcv.at[5])

time: 71 us -> 70.2 us (0.989)
    pallas_call x1, Pallas kernels: 69.4 us -> 68.7 us  [shards(): pl.pallas_call(kernel, out_shape=jax.ShapeDtypeStruct((2, NS, 64), F32),...]
where the time goes in v5:
time: 70.2 us; the launch traced here: 70.1 us
  Pallas kernels  68.7 us (98%)
  other arithmetic  1.37 us (2%)
    pallas_call x1, Pallas kernels, shards(): pl.pallas_call(kernel, out_shape=jax.ShapeDtypeStruct((2, NS, 64), F32),...  68.7 us

profile of v5, /device:TPU:1, one launch (start us, length us, event | category | flops | bytes accessed | tf_op | source)
XLA Modules:
  0.0 70.1 jit_solution(1533148228327033727)
XLA Ops:
  0.0 68.7 %shard_map.118 = f32[2,32,64]{2,1,0:T(8,128)} custom-call(s32[32]{0:T(128)} %lengths_hbm.1, s32[32]{0:T(128)} %slot_hbm.1, bf16[3,256]{1,0:T(4,128)(2,1)} %bitcast.8, bf16[2,1024]{1,0:T(2,128)(2,1)} %bitcast.7, s32[32,256]{1,0:T(8,128)} %table_hbm.1, bf16[2,32,512]{2,1,0:T(8,128)(2,1)} %residual_hbm.1, f32[1,512]{1,0:T(1,128)} %bitcast.9, ...), custom_call_target="tpu_custom_call" | custom-call | tf_op jit(solution)/shard_map/pallas_call | solution.py:563
  68.7 1.4 %convert_element_type.3 = bf16[2,32,64]{2,1,0:T(8,128)(2,1)} convert(f32[2,32,64]{2,1,0:T(8,128)} %shard_map.118) | non-fusion elementwise | flops 4096 | bytes 24576 | tf_op jit(solution)/shard_map/convert_element_type | solution.py:590
